TPU v7x, 512 devices: a whole 4x4x16 slice. The times are simulated.
512 devices in a mesh: win: 16 (over y, x), tile: 32 (over z, core).
Axes of the slice: x: 4, y: 4, z: 16, core: 2. Of those that a mesh axis runs over, the one named last changes fastest.
Arguments:
- traj_start: float32 [16, 3, 2, 256, 1024], P('win', None, None, 'tile'), may hold values from -3 to 3
- forcing: float32 [3, 2, 256, 1024], P(None, None, 'tile'), may hold values from -3 to 3
- depth: float32 [2, 256, 1024], P(None, 'tile'), may hold values from 0.5 to 2
- obs_step: int32 [16, 256, 1024], P('win', 'tile'), may hold values from 0 to 6
- obs_value: float32 [16, 2, 256, 1024], P('win', None, 'tile'), may hold values from -4 to 4
- obs_weight: float32 [256, 1024], P('tile'), may hold values from 0.5 to 2
- error_weight: float32 [3, 2], replicated, may hold values from 0.5 to 2
Outputs:
- grad_start: float32 [16, 3, 2, 256, 1024], P('win', None, None, 'tile')
- grad_forcing: float32 [3, 2, 256, 1024], P(None, None, 'tile')
Inputs may be any that keep to these rules, and one draw needn't show every extreme that they name: `obs_step`: 0 means that the cell is not observed in that sub-window; k >= 1 means that its thicknesses are observed after step k.
All inputs are finite; a program needn't handle non-finite values.
Results may differ from a plain program's by a relative error of at most 0.0003.
Values sent between devices are 32-bit elements; how exact they have to be, the bound alone decides.
A program may use at most 64 MiB of HBM per device.

v0:
```python
import jax
import jax.numpy as jnp
from jax import lax
from jax.sharding import PartitionSpec as P

STEPS = 6
LAT_ROWS = 2048


C_STEP = 0.2


def padded_2(block, sides, width):
    for axis, dim in sides:
        count = lax.axis_size(axis)
        forward = [(i, i + 1) for i in range(count - 1)]
        backward = [(target, source) for source, target in forward]
        low = lax.ppermute(
            lax.slice_in_dim(block, block.shape[dim] - width, None, axis=dim), axis, forward
        )
        high = lax.ppermute(lax.slice_in_dim(block, 0, width, axis=dim), axis, backward)
        block = jnp.concatenate([low, block, high], axis=dim)
    return block


def shifted(array, axis, by):
    count = lax.axis_size(axis)
    pairs = [(i, i + by) for i in range(count) if 0 <= i + by < count]
    return lax.ppermute(array, axis, pairs)


def along_x(field):
    return 0.5 * (jnp.roll(field, -1, axis=-1) - jnp.roll(field, 1, axis=-1))


def along_y(field):
    return 0.5 * (field[:, 2:] - field[:, :-2])


def advance(padded, depth_pad, first_row, total_rows):
    zonal = padded[0]
    meridional = padded[1]
    height = padded[2]
    pressure = jnp.cumsum(height, axis=0)
    inner_rows = padded.shape[2] - 2
    latitude_rows = (first_row + 1 + jnp.arange(inner_rows, dtype=jnp.int32)).astype(jnp.float32)
    coriolis = (2.0 * jnp.sin(jnp.pi * ((latitude_rows + 0.5) / total_rows - 0.5)))[None, :, None]
    zonal_in = zonal[:, 1:-1]
    merid_in = meridional[:, 1:-1]
    height_in = height[:, 1:-1]
    column_mass = depth_pad + height
    new_zonal = (
        zonal_in
        - C_STEP
        * (zonal_in * along_x(zonal_in) + merid_in * along_y(zonal) + along_x(pressure[:, 1:-1]))
        + C_STEP * coriolis * merid_in
    )
    new_merid = (
        merid_in
        - C_STEP
        * (zonal_in * along_x(merid_in) + merid_in * along_y(meridional) + along_y(pressure))
        - C_STEP * coriolis * zonal_in
    )
    new_height = height_in - C_STEP * (
        along_x((column_mass * zonal)[:, 1:-1]) + along_y(column_mass * meridional)
    )
    return jnp.stack([new_zonal, new_merid, new_height])


def local(traj_start, forcing, depth, obs_step, obs_value, obs_weight, error_weight):
    initial = traj_start[0]
    local_rows = initial.shape[2]
    total_rows = local_rows * lax.axis_size("tile")
    band_offset = (LAT_ROWS - total_rows) // 2
    base_row = lax.axis_index("tile") * local_rows
    history = []
    depth_pad = padded_2(depth, (("tile", 1),), 1)
    current = initial
    for step_index in range(STEPS):
        padded = padded_2(current, (("tile", 2),), 1)
        history.append(padded)
        current = advance(padded, depth_pad, band_offset + base_row - 1, LAT_ROWS) + forcing
    upcoming = shifted(initial, "win", -1)
    is_last = lax.axis_index("win") == lax.axis_size("win") - 1
    weights = error_weight[:, :, None, None]
    misfit = jnp.where(is_last, 0.0, weights * (upcoming - current))
    earlier = shifted(misfit, "win", 1)
    adjoint = -misfit
    forcing_grad = jnp.zeros_like(adjoint)
    observed = obs_step[0]
    measured = obs_value[0]

    def plain_step(padded):
        return advance(padded, depth_pad, band_offset + base_row - 1, LAT_ROWS)

    for step_index in range(STEPS, 0, -1):
        if step_index == STEPS:
            state_now = current
        else:
            state_now = history[step_index][:, :, 1:-1]
        selected = (observed == step_index).astype(jnp.float32)
        pull_obs = obs_weight * selected * (state_now[2] - measured)
        adjoint = jnp.concatenate([adjoint[:2], (adjoint[2] + pull_obs)[None]], axis=0)
        forcing_grad = forcing_grad + adjoint
        unused, backward = jax.vjp(plain_step, history[step_index - 1])
        (cotangent,) = backward(adjoint)
        rims = jnp.concatenate([cotangent[:, :, :1], cotangent[:, :, -1:]], axis=2)
        arrived = padded_2(rims, (("tile", 2),), 1)
        middle = jnp.zeros(
            (cotangent.shape[0], cotangent.shape[1], local_rows - 2, cotangent.shape[3]),
            jnp.float32,
        )
        adjoint = cotangent[:, :, 1:-1] + jnp.concatenate(
            [arrived[:, :, :1], middle, arrived[:, :, 3:]], axis=2
        )
    grad_start = (adjoint + earlier)[None]
    grad_forcing = lax.psum(forcing_grad, "win")
    return (grad_start, grad_forcing)


def solution(mesh):
    return jax.shard_map(
        local,
        mesh=mesh,
        in_specs=(
            P("win", None, None, "tile", None),
            P(None, None, "tile", None),
            P(None, "tile", None),
            P("win", "tile", None),
            P("win", None, "tile", None),
            P("tile", None),
            P(),
        ),
        out_specs=(P("win", None, None, "tile", None), P(None, None, "tile", None)),
        check_vma=False,
    )
```

profile of v0, /device:TPU:1, one launch (start us, length us, event | category | flops | bytes accessed | tf_op | source)
XLA Modules:
  0.0 273.7 jit_solution(7625607350761797202)
XLA Ops:
  7.2 1.1 fusion.300
  8.3 8.8 %collective-permute-start.2 = (f32[3,2,1,1024]{3,2,1,0:T(1,128)S(1)}, f32[3,2,1,1024]{3,2,1,0:T(1,128)S(1)}, u32[]{:S(2)}, u32[]{:S(2)}) collective-permute-start(f32[3,2,1,1024]{3,2,1,0:T(1,128)S(1)} %get-tuple-element.238), channel_id=1, source_target_pairs={{1,0},{2,1},{3,2},{4,3},{5,4},{6,5},{7,6},{8,7},{9,8},{10,9},{11,1... | collective-permute-start | bytes 73736 | tf_op jit(solution)/shard_map/ppermute | solution.py:21
  17.1 1.9 collective-permute-start.1
  19.0 2.4 collective-permute-start.4
  21.4 3.2 %collective-permute-start.3 = (f32[2,1,1024]{2,1,0:T(1,128)S(1)}, f32[2,1,1024]{2,1,0:T(1,128)S(1)}, u32[]{:S(2)}, u32[]{:S(2)}) collective-permute-start(f32[2,1,1024]{2,1,0:T(1,128)S(1)} %get-tuple-element.347), channel_id=1, source_target_pairs={{0,1},{1,2},{2,3},{3,4},{4,5},{5,6},{6,7},{7,8},{8,9},{9,10},{10,1... | collective-permute-start | bytes 24584 | tf_op jit(solution)/shard_map/ppermute | solution.py:18
  24.7 1.0 pad_maximum_fusion
  26.5 0.5 copy-done.102
  27.3 0.8 copy-done.1
  28.1 1.9 collective-permute-start.6
  30.1 3.8 %collective-permute-start.5 = (f32[3,2,1,1024]{3,2,1,0:T(1,128)S(1)}, f32[3,2,1,1024]{3,2,1,0:T(1,128)S(1)}, u32[]{:S(2)}, u32[]{:S(2)}) collective-permute-start(f32[3,2,1,1024]{3,2,1,0:T(1,128)S(1)} %get-tuple-element.235), channel_id=1, source_target_pairs={{0,1},{1,2},{2,3},{3,4},{4,5},{5,6},{6,7},{7,8},{8,9},{9,10},{10,1... | collective-permute-start | bytes 73736 | tf_op jit(solution)/shard_map/ppermute | solution.py:18
  33.9 0.9 collective-permute-done.5
  36.6 1.9 collective-permute-start.8
  38.5 4.2 %collective-permute-start.7 = (f32[3,2,1,1024]{3,2,1,0:T(1,128)S(1)}, f32[3,2,1,1024]{3,2,1,0:T(1,128)S(1)}, u32[]{:S(2)}, u32[]{:S(2)}) collective-permute-start(f32[3,2,1,1024]{3,2,1,0:T(1,128)S(1)} %get-tuple-element.233), channel_id=1, source_target_pairs={{0,1},{1,2},{2,3},{3,4},{4,5},{5,6},{6,7},{7,8},{8,9},{9,10},{10,1... | collective-permute-start | bytes 73736 | tf_op jit(solution)/shard_map/ppermute | solution.py:18
  42.8 0.9 collective-permute-done.7
  45.5 1.9 collective-permute-start.10
  47.4 4.2 %collective-permute-start.9 = (f32[3,2,1,1024]{3,2,1,0:T(1,128)S(1)}, f32[3,2,1,1024]{3,2,1,0:T(1,128)S(1)}, u32[]{:S(2)}, u32[]{:S(2)}) collective-permute-start(f32[3,2,1,1024]{3,2,1,0:T(1,128)S(1)} %get-tuple-element.231), channel_id=1, source_target_pairs={{0,1},{1,2},{2,3},{3,4},{4,5},{5,6},{6,7},{7,8},{8,9},{9,10},{10,1... | collective-permute-start | bytes 73736 | tf_op jit(solution)/shard_map/ppermute | solution.py:18
  51.6 0.9 collective-permute-done.9
  54.3 1.9 collective-permute-start.12
  56.2 4.2 %collective-permute-start.11 = (f32[3,2,1,1024]{3,2,1,0:T(1,128)S(1)}, f32[3,2,1,1024]{3,2,1,0:T(1,128)S(1)}, u32[]{:S(2)}, u32[]{:S(2)}) collective-permute-start(f32[3,2,1,1024]{3,2,1,0:T(1,128)S(1)} %get-tuple-element.229), channel_id=1, source_target_pairs={{0,1},{1,2},{2,3},{3,4},{4,5},{5,6},{6,7},{7,8},{8,9},{9,10},{10,1... | collective-permute-start | bytes 73736 | tf_op jit(solution)/shard_map/ppermute | solution.py:18
  60.5 1.3 collective-permute-start
  63.5 0.7 copy-done.16
  64.2 0.6 fusion.295
  64.8 1.9 collective-permute-start.14
  66.8 3.8 %collective-permute-start.13 = (f32[3,2,1,1024]{3,2,1,0:T(1,128)}, f32[3,2,1,1024]{3,2,1,0:T(1,128)}, u32[]{:S(2)}, u32[]{:S(2)}) collective-permute-start(f32[3,2,1,1024]{3,2,1,0:T(1,128)} %get-tuple-element.227), channel_id=1, source_target_pairs={{0,1},{1,2},{2,3},{3,4},{4,5},{5,6},{6,7},{7,8},{8,9},{9,10},{10,1... | collective-permute-start | bytes 73736 | tf_op jit(solution)/shard_map/ppermute | solution.py:18
  70.6 0.7 bitcast_select_fusion.5
  71.3 1.3 copy.9
  72.7 1.0 pad_maximum_fusion.5
  74.6 0.6 copy-done.65
  75.6 0.5 copy-done.110
  76.1 1.7 fusion.294
  79.0 0.2 fusion
  79.4 1.9 collective-permute-start.16
  81.3 3.6 %collective-permute-start.15 = (f32[3,2,1,1024]{3,2,1,0:T(1,128)S(1)}, f32[3,2,1,1024]{3,2,1,0:T(1,128)S(1)}, u32[]{:S(2)}, u32[]{:S(2)}) collective-permute-start(f32[3,2,1,1024]{3,2,1,0:T(1,128)S(1)} %get-tuple-element.99), channel_id=1, source_target_pairs={{0,1},{1,2},{2,3},{3,4},{4,5},{5,6},{6,7},{7,8},{8,9},{9,10},{10,1... | collective-permute-start | bytes 73736 | tf_op jit(solution)/shard_map/ppermute | solution.py:18
  85.1 4.6 %collective-permute-start.27 = (f32[3,2,8,1024]{3,2,1,0:T(8,128)}, f32[3,2,8,1024]{3,2,1,0:T(8,128)}, u32[]{:S(2)}, u32[]{:S(2)}) collective-permute-start(f32[3,2,8,1024]{3,2,1,0:T(8,128)} %get-tuple-element.63), channel_id=1, source_target_pairs={{0,32},{32,64},{64,96},{96,128},{128,160},{160,192},{192,224},{224... | collective-permute-start | bytes 589832 | tf_op jit(solution)/shard_map/ppermute | solution.py:29
  90.7 0.5 copy-done.51
  91.7 0.2 fusion.1
  92.1 1.9 collective-permute-start.18
  94.1 3.6 %collective-permute-start.17 = (f32[3,2,1,1024]{3,2,1,0:T(1,128)S(1)}, f32[3,2,1,1024]{3,2,1,0:T(1,128)S(1)}, u32[]{:S(2)}, u32[]{:S(2)}) collective-permute-start(f32[3,2,1,1024]{3,2,1,0:T(1,128)S(1)} %get-tuple-element.97), channel_id=1, source_target_pairs={{0,1},{1,2},{2,3},{3,4},{4,5},{5,6},{6,7},{7,8},{8,9},{9,10},{10,1... | collective-permute-start | bytes 73736 | tf_op jit(solution)/shard_map/ppermute | solution.py:18
  97.8 0.9 collective-permute-done.17
  99.7 0.5 copy-done.43
  100.6 0.2 fusion.2
  101.1 1.9 collective-permute-start.20
  103.0 4.2 %collective-permute-start.19 = (f32[3,2,1,1024]{3,2,1,0:T(1,128)S(1)}, f32[3,2,1,1024]{3,2,1,0:T(1,128)S(1)}, u32[]{:S(2)}, u32[]{:S(2)}) collective-permute-start(f32[3,2,1,1024]{3,2,1,0:T(1,128)S(1)} %get-tuple-element.95), channel_id=1, source_target_pairs={{0,1},{1,2},{2,3},{3,4},{4,5},{5,6},{6,7},{7,8},{8,9},{9,10},{10,1... | collective-permute-start | bytes 73736 | tf_op jit(solution)/shard_map/ppermute | solution.py:18
  107.3 0.9 collective-permute-done.19
  109.1 0.2 copy-done.83
  110.1 0.2 fusion.3
  110.5 1.9 collective-permute-start.22
  112.5 4.2 %collective-permute-start.21 = (f32[3,2,1,1024]{3,2,1,0:T(1,128)S(1)}, f32[3,2,1,1024]{3,2,1,0:T(1,128)S(1)}, u32[]{:S(2)}, u32[]{:S(2)}) collective-permute-start(f32[3,2,1,1024]{3,2,1,0:T(1,128)S(1)} %get-tuple-element.93), channel_id=1, source_target_pairs={{0,1},{1,2},{2,3},{3,4},{4,5},{5,6},{6,7},{7,8},{8,9},{9,10},{10,1... | collective-permute-start | bytes 73736 | tf_op jit(solution)/shard_map/ppermute | solution.py:18
  116.8 0.9 collective-permute-done.21
  118.6 0.2 copy-done.75
  119.6 0.2 fusion.4
  120.0 1.9 collective-permute-start.24
  122.0 4.2 %collective-permute-start.23 = (f32[3,2,1,1024]{3,2,1,0:T(1,128)S(1)}, f32[3,2,1,1024]{3,2,1,0:T(1,128)S(1)}, u32[]{:S(2)}, u32[]{:S(2)}) collective-permute-start(f32[3,2,1,1024]{3,2,1,0:T(1,128)S(1)} %get-tuple-element.91), channel_id=1, source_target_pairs={{0,1},{1,2},{2,3},{3,4},{4,5},{5,6},{6,7},{7,8},{8,9},{9,10},{10,1... | collective-permute-start | bytes 73736 | tf_op jit(solution)/shard_map/ppermute | solution.py:18
  126.2 0.9 collective-permute-done.23
  128.3 0.3 copy-done.103
  128.6 0.2 copy-done.55
  129.3 0.2 fusion.5
  129.7 1.9 collective-permute-start.26
  131.7 4.3 %collective-permute-start.25 = (f32[3,2,1,1024]{3,2,1,0:T(1,128)S(1)}, f32[3,2,1,1024]{3,2,1,0:T(1,128)S(1)}, u32[]{:S(2)}, u32[]{:S(2)}) collective-permute-start(f32[3,2,1,1024]{3,2,1,0:T(1,128)S(1)} %get-tuple-element.89), channel_id=1, source_target_pairs={{0,1},{1,2},{2,3},{3,4},{4,5},{5,6},{6,7},{7,8},{8,9},{9,10},{10,1... | collective-permute-start | bytes 73736 | tf_op jit(solution)/shard_map/ppermute | solution.py:18
  136.1 0.8 fusion.11
  136.9 0.6 copy-done.109
  137.5 1.7 fusion.7
  139.2 126.0 %all-reduce.194.cloned.1.call-done = f32[3,2,8,1024]{3,2,1,0:T(8,128)} async-done(((f32[3,2,8,1024]{3,2,1,0:T(8,128)}), f32[3,2,8,1024]{3,2,1,0:T(8,128)}) %all-reduce.194.cloned.1.call-update) | async-done | bytes 196624 | tf_op jit(solution)/shard_map/psum | solution.py:117
  265.2 1.6 copy.11
  (474 shorter events, 18.9 us)
Async XLA Ops:
  7.2 11.8 %copy-start = (f32[2,8,1024]{2,1,0:T(8,128)S(1)}, f32[2,8,1024]{2,1,0:T(8,128)}, u32[]{:S(2)}) copy-start(f32[2,8,1024]{2,1,0:T(8,128)} %param.9) | copy-start | bytes 196612
  7.2 258.0 %all-reduce.194.cloned.1.call-start = ((), (), s32[]{:S(2)}) async-start(), calls=%async_computation | async-start | bytes 393216 | tf_op jit(solution)/shard_map/psum | solution.py:117
  8.3 16.4 %collective-permute-start.2 = (f32[3,2,1,1024]{3,2,1,0:T(1,128)S(1)}, f32[3,2,1,1024]{3,2,1,0:T(1,128)S(1)}, u32[]{:S(2)}, u32[]{:S(2)}) collective-permute-start(f32[3,2,1,1024]{3,2,1,0:T(1,128)S(1)} %get-tuple-element.238), channel_id=1, source_target_pairs={{1,0},{2,1},{3,2},{4,3},{5,4},{6,5},{7,6},{8,7},{9,8},{10,9},{11,1... | collective-permute-start | bytes 73736 | tf_op jit(solution)/shard_map/ppermute | solution.py:21
  17.1 7.6 %collective-permute-start.1 = (f32[3,2,1,1024]{3,2,1,0:T(1,128)S(1)}, f32[3,2,1,1024]{3,2,1,0:T(1,128)S(1)}, u32[]{:S(2)}, u32[]{:S(2)}) collective-permute-start(f32[3,2,1,1024]{3,2,1,0:T(1,128)S(1)} %get-tuple-element.237), channel_id=1, source_target_pairs={{0,1},{1,2},{2,3},{3,4},{4,5},{5,6},{6,7},{7,8},{8,9},{9,10},{10,1... | collective-permute-start | bytes 73736 | tf_op jit(solution)/shard_map/ppermute | solution.py:18
  19.0 6.7 %collective-permute-start.4 = (f32[2,1,1024]{2,1,0:T(1,128)S(1)}, f32[2,1,1024]{2,1,0:T(1,128)S(1)}, u32[]{:S(2)}, u32[]{:S(2)}) collective-permute-start(f32[2,1,1024]{2,1,0:T(1,128)S(1)} %get-tuple-element.348), channel_id=1, source_target_pairs={{1,0},{2,1},{3,2},{4,3},{5,4},{6,5},{7,6},{8,7},{9,8},{10,9},{11,1... | collective-permute-start | bytes 24584 | tf_op jit(solution)/shard_map/ppermute | solution.py:21
  21.4 4.3 %collective-permute-start.3 = (f32[2,1,1024]{2,1,0:T(1,128)S(1)}, f32[2,1,1024]{2,1,0:T(1,128)S(1)}, u32[]{:S(2)}, u32[]{:S(2)}) collective-permute-start(f32[2,1,1024]{2,1,0:T(1,128)S(1)} %get-tuple-element.347), channel_id=1, source_target_pairs={{0,1},{1,2},{2,3},{3,4},{4,5},{5,6},{6,7},{7,8},{8,9},{9,10},{10,1... | collective-permute-start | bytes 24584 | tf_op jit(solution)/shard_map/ppermute | solution.py:18
  24.7 38.5 %copy-start.64 = (f32[8]{0:T(128)}, f32[8]{0:T(128)S(1)}, u32[]{:S(2)}) copy-start(f32[8]{0:T(128)S(1)} %sine_multiply_fusion) | copy-start | bytes 100
  26.2 0.9 copy-start.18
  26.2 0.9 copy-start.20
  27.1 0.9 copy-start.1
  28.1 6.7 %copy-start.8 = (f32[3,2,8,1024]{3,2,1,0:T(8,128)}, f32[3,2,8,1024]{3,2,1,0:T(8,128)S(1)}, u32[]{:S(2)}) copy-start(f32[3,2,8,1024]{3,2,1,0:T(8,128)S(1)} %maximum_add_fusion) | copy-start | bytes 589828
  28.1 5.8 %collective-permute-start.6 = (f32[3,2,1,1024]{3,2,1,0:T(1,128)S(1)}, f32[3,2,1,1024]{3,2,1,0:T(1,128)S(1)}, u32[]{:S(2)}, u32[]{:S(2)}) collective-permute-start(f32[3,2,1,1024]{3,2,1,0:T(1,128)S(1)} %get-tuple-element.236), channel_id=1, source_target_pairs={{1,0},{2,1},{3,2},{4,3},{5,4},{6,5},{7,6},{8,7},{9,8},{10,9},{11,1... | collective-permute-start | bytes 73736 | tf_op jit(solution)/shard_map/ppermute | solution.py:21
  30.1 4.7 %collective-permute-start.5 = (f32[3,2,1,1024]{3,2,1,0:T(1,128)S(1)}, f32[3,2,1,1024]{3,2,1,0:T(1,128)S(1)}, u32[]{:S(2)}, u32[]{:S(2)}) collective-permute-start(f32[3,2,1,1024]{3,2,1,0:T(1,128)S(1)} %get-tuple-element.235), channel_id=1, source_target_pairs={{0,1},{1,2},{2,3},{3,4},{4,5},{5,6},{6,7},{7,8},{8,9},{9,10},{10,1... | collective-permute-start | bytes 73736 | tf_op jit(solution)/shard_map/ppermute | solution.py:18
  36.5 7.1 %copy-start.10 = (f32[3,2,8,1024]{3,2,1,0:T(8,128)}, f32[3,2,8,1024]{3,2,1,0:T(8,128)S(1)}, u32[]{:S(2)}) copy-start(f32[3,2,8,1024]{3,2,1,0:T(8,128)S(1)} %maximum_add_fusion.1) | copy-start | bytes 589828
  36.6 6.2 %collective-permute-start.8 = (f32[3,2,1,1024]{3,2,1,0:T(1,128)S(1)}, f32[3,2,1,1024]{3,2,1,0:T(1,128)S(1)}, u32[]{:S(2)}, u32[]{:S(2)}) collective-permute-start(f32[3,2,1,1024]{3,2,1,0:T(1,128)S(1)} %get-tuple-element.234), channel_id=1, source_target_pairs={{1,0},{2,1},{3,2},{4,3},{5,4},{6,5},{7,6},{8,7},{9,8},{10,9},{11,1... | collective-permute-start | bytes 73736 | tf_op jit(solution)/shard_map/ppermute | solution.py:21
  38.5 5.1 %collective-permute-start.7 = (f32[3,2,1,1024]{3,2,1,0:T(1,128)S(1)}, f32[3,2,1,1024]{3,2,1,0:T(1,128)S(1)}, u32[]{:S(2)}, u32[]{:S(2)}) collective-permute-start(f32[3,2,1,1024]{3,2,1,0:T(1,128)S(1)} %get-tuple-element.233), channel_id=1, source_target_pairs={{0,1},{1,2},{2,3},{3,4},{4,5},{5,6},{6,7},{7,8},{8,9},{9,10},{10,1... | collective-permute-start | bytes 73736 | tf_op jit(solution)/shard_map/ppermute | solution.py:18
  45.4 7.1 %copy-start.12 = (f32[3,2,8,1024]{3,2,1,0:T(8,128)}, f32[3,2,8,1024]{3,2,1,0:T(8,128)S(1)}, u32[]{:S(2)}) copy-start(f32[3,2,8,1024]{3,2,1,0:T(8,128)S(1)} %maximum_add_fusion.2) | copy-start | bytes 589828
  45.5 6.2 %collective-permute-start.10 = (f32[3,2,1,1024]{3,2,1,0:T(1,128)S(1)}, f32[3,2,1,1024]{3,2,1,0:T(1,128)S(1)}, u32[]{:S(2)}, u32[]{:S(2)}) collective-permute-start(f32[3,2,1,1024]{3,2,1,0:T(1,128)S(1)} %get-tuple-element.232), channel_id=1, source_target_pairs={{1,0},{2,1},{3,2},{4,3},{5,4},{6,5},{7,6},{8,7},{9,8},{10,9},{11,1... | collective-permute-start | bytes 73736 | tf_op jit(solution)/shard_map/ppermute | solution.py:21
  47.4 5.1 %collective-permute-start.9 = (f32[3,2,1,1024]{3,2,1,0:T(1,128)S(1)}, f32[3,2,1,1024]{3,2,1,0:T(1,128)S(1)}, u32[]{:S(2)}, u32[]{:S(2)}) collective-permute-start(f32[3,2,1,1024]{3,2,1,0:T(1,128)S(1)} %get-tuple-element.231), channel_id=1, source_target_pairs={{0,1},{1,2},{2,3},{3,4},{4,5},{5,6},{6,7},{7,8},{8,9},{9,10},{10,1... | collective-permute-start | bytes 73736 | tf_op jit(solution)/shard_map/ppermute | solution.py:18
  54.2 7.6 %copy-start.14 = (f32[3,2,8,1024]{3,2,1,0:T(8,128)}, f32[3,2,8,1024]{3,2,1,0:T(8,128)S(1)}, u32[]{:S(2)}) copy-start(f32[3,2,8,1024]{3,2,1,0:T(8,128)S(1)} %maximum_add_fusion.3) | copy-start | bytes 589828
  54.3 7.5 %collective-permute-start.12 = (f32[3,2,1,1024]{3,2,1,0:T(1,128)S(1)}, f32[3,2,1,1024]{3,2,1,0:T(1,128)S(1)}, u32[]{:S(2)}, u32[]{:S(2)}) collective-permute-start(f32[3,2,1,1024]{3,2,1,0:T(1,128)S(1)} %get-tuple-element.230), channel_id=1, source_target_pairs={{1,0},{2,1},{3,2},{4,3},{5,4},{6,5},{7,6},{8,7},{9,8},{10,9},{11,1... | collective-permute-start | bytes 73736 | tf_op jit(solution)/shard_map/ppermute | solution.py:21
  56.2 5.5 %collective-permute-start.11 = (f32[3,2,1,1024]{3,2,1,0:T(1,128)S(1)}, f32[3,2,1,1024]{3,2,1,0:T(1,128)S(1)}, u32[]{:S(2)}, u32[]{:S(2)}) collective-permute-start(f32[3,2,1,1024]{3,2,1,0:T(1,128)S(1)} %get-tuple-element.229), channel_id=1, source_target_pairs={{0,1},{1,2},{2,3},{3,4},{4,5},{5,6},{6,7},{7,8},{8,9},{9,10},{10,1... | collective-permute-start | bytes 73736 | tf_op jit(solution)/shard_map/ppermute | solution.py:18
  60.5 15.1 %collective-permute-start = (f32[3,2,8,1024]{3,2,1,0:T(8,128)}, f32[3,2,8,1024]{3,2,1,0:T(8,128)}, u32[]{:S(2)}, u32[]{:S(2)}) collective-permute-start(f32[3,2,8,1024]{3,2,1,0:T(8,128)} %bitcast), channel_id=1, source_target_pairs={{32,0},{64,32},{96,64},{128,96},{160,128},{192,160},{224,192},{256... | collective-permute-start | bytes 589832 | tf_op jit(solution)/shard_map/ppermute | solution.py:29
  64.2 6.4 %copy-start.106 = (f32[8,1024]{1,0:T(8,128)S(1)}, f32[8,1024]{1,0:T(8,128)}, u32[]{:S(2)}) copy-start(f32[8,1024]{1,0:T(8,128)} %param.12) | copy-start | bytes 98308
  64.2 6.4 %copy-start.107 = (s32[1,8,1024]{2,1,0:T(8,128)S(1)}, s32[1,8,1024]{2,1,0:T(8,128)}, u32[]{:S(2)}) copy-start(s32[1,8,1024]{2,1,0:T(8,128)} %param.10) | copy-start | bytes 98308
  64.8 7.9 %collective-permute-start.14 = (f32[3,2,1,1024]{3,2,1,0:T(1,128)}, f32[3,2,1,1024]{3,2,1,0:T(1,128)}, u32[]{:S(2)}, u32[]{:S(2)}) collective-permute-start(f32[3,2,1,1024]{3,2,1,0:T(1,128)} %get-tuple-element.228), channel_id=1, source_target_pairs={{1,0},{2,1},{3,2},{4,3},{5,4},{6,5},{7,6},{8,7},{9,8},{10,9},{11,1... | collective-permute-start | bytes 73736 | tf_op jit(solution)/shard_map/ppermute | solution.py:21
  66.8 6.0 %collective-permute-start.13 = (f32[3,2,1,1024]{3,2,1,0:T(1,128)}, f32[3,2,1,1024]{3,2,1,0:T(1,128)}, u32[]{:S(2)}, u32[]{:S(2)}) collective-permute-start(f32[3,2,1,1024]{3,2,1,0:T(1,128)} %get-tuple-element.227), channel_id=1, source_target_pairs={{0,1},{1,2},{2,3},{3,4},{4,5},{5,6},{6,7},{7,8},{8,9},{9,10},{10,1... | collective-permute-start | bytes 73736 | tf_op jit(solution)/shard_map/ppermute | solution.py:18
  72.7 54.4 %copy-start.108 = (f32[8]{0:T(128)}, f32[8]{0:T(128)S(1)}, u32[]{:S(2)}) copy-start(f32[8]{0:T(128)S(1)} %pad.800.clone) | copy-start | bytes 100
  75.6 2.3 copy-start.7
  75.6 2.3 copy-start.58
  79.4 10.3 %collective-permute-start.16 = (f32[3,2,1,1024]{3,2,1,0:T(1,128)S(1)}, f32[3,2,1,1024]{3,2,1,0:T(1,128)S(1)}, u32[]{:S(2)}, u32[]{:S(2)}) collective-permute-start(f32[3,2,1,1024]{3,2,1,0:T(1,128)S(1)} %get-tuple-element.100), channel_id=1, source_target_pairs={{1,0},{2,1},{3,2},{4,3},{5,4},{6,5},{7,6},{8,7},{9,8},{10,9},{11,1... | collective-permute-start | bytes 73736 | tf_op jit(solution)/shard_map/ppermute | solution.py:21
  81.3 8.4 %collective-permute-start.15 = (f32[3,2,1,1024]{3,2,1,0:T(1,128)S(1)}, f32[3,2,1,1024]{3,2,1,0:T(1,128)S(1)}, u32[]{:S(2)}, u32[]{:S(2)}) collective-permute-start(f32[3,2,1,1024]{3,2,1,0:T(1,128)S(1)} %get-tuple-element.99), channel_id=1, source_target_pairs={{0,1},{1,2},{2,3},{3,4},{4,5},{5,6},{6,7},{7,8},{8,9},{9,10},{10,1... | collective-permute-start | bytes 73736 | tf_op jit(solution)/shard_map/ppermute | solution.py:18
  85.0 4.8 %copy-start.17 = (f32[3,2,8,1024]{3,2,1,0:T(8,128)S(1)}, f32[3,2,8,1024]{3,2,1,0:T(8,128)}, u32[]{:S(2)}) copy-start(f32[3,2,8,1024]{3,2,1,0:T(8,128)} %copy-done.16) | copy-start | bytes 589828
  85.1 4.8 %copy-start.61 = (f32[8,1024]{1,0:T(8,128)S(1)}, f32[8,1024]{1,0:T(8,128)}, u32[]{:S(2)}) copy-start(f32[8,1024]{1,0:T(8,128)} %get-tuple-element.344) | copy-start | bytes 98308
  85.1 51.9 %collective-permute-start.27 = (f32[3,2,8,1024]{3,2,1,0:T(8,128)}, f32[3,2,8,1024]{3,2,1,0:T(8,128)}, u32[]{:S(2)}, u32[]{:S(2)}) collective-permute-start(f32[3,2,8,1024]{3,2,1,0:T(8,128)} %get-tuple-element.63), channel_id=1, source_target_pairs={{0,32},{32,64},{64,96},{96,128},{128,160},{160,192},{192,224},{224... | collective-permute-start | bytes 589832 | tf_op jit(solution)/shard_map/ppermute | solution.py:29
  89.8 38.0 %copy-start.2 = (f32[3,2,8,1024]{3,2,1,0:T(8,128)}, f32[3,2,8,1024]{3,2,1,0:T(8,128)S(1)}, u32[]{:S(2)}) copy-start(f32[3,2,8,1024]{3,2,1,0:T(8,128)S(1)} %slice_add_fusion.5) | copy-start | bytes 589828
  92.1 5.6 %collective-permute-start.18 = (f32[3,2,1,1024]{3,2,1,0:T(1,128)S(1)}, f32[3,2,1,1024]{3,2,1,0:T(1,128)S(1)}, u32[]{:S(2)}, u32[]{:S(2)}) collective-permute-start(f32[3,2,1,1024]{3,2,1,0:T(1,128)S(1)} %get-tuple-element.98), channel_id=1, source_target_pairs={{1,0},{2,1},{3,2},{4,3},{5,4},{6,5},{7,6},{8,7},{9,8},{10,9},{11,1... | collective-permute-start | bytes 73736 | tf_op jit(solution)/shard_map/ppermute | solution.py:21
  94.1 4.6 %collective-permute-start.17 = (f32[3,2,1,1024]{3,2,1,0:T(1,128)S(1)}, f32[3,2,1,1024]{3,2,1,0:T(1,128)S(1)}, u32[]{:S(2)}, u32[]{:S(2)}) collective-permute-start(f32[3,2,1,1024]{3,2,1,0:T(1,128)S(1)} %get-tuple-element.97), channel_id=1, source_target_pairs={{0,1},{1,2},{2,3},{3,4},{4,5},{5,6},{6,7},{7,8},{8,9},{9,10},{10,1... | collective-permute-start | bytes 73736 | tf_op jit(solution)/shard_map/ppermute | solution.py:18
  97.7 1.0 copy-start.15
  97.8 1.0 copy-start.60
  98.7 29.1 %copy-start.3 = (f32[3,2,8,1024]{3,2,1,0:T(8,128)}, f32[3,2,8,1024]{3,2,1,0:T(8,128)S(1)}, u32[]{:S(2)}) copy-start(f32[3,2,8,1024]{3,2,1,0:T(8,128)S(1)} %slice_add_fusion.4) | copy-start | bytes 589828
  101.1 6.2 %collective-permute-start.20 = (f32[3,2,1,1024]{3,2,1,0:T(1,128)S(1)}, f32[3,2,1,1024]{3,2,1,0:T(1,128)S(1)}, u32[]{:S(2)}, u32[]{:S(2)}) collective-permute-start(f32[3,2,1,1024]{3,2,1,0:T(1,128)S(1)} %get-tuple-element.96), channel_id=1, source_target_pairs={{1,0},{2,1},{3,2},{4,3},{5,4},{6,5},{7,6},{8,7},{9,8},{10,9},{11,1... | collective-permute-start | bytes 73736 | tf_op jit(solution)/shard_map/ppermute | solution.py:21
  103.0 5.1 %collective-permute-start.19 = (f32[3,2,1,1024]{3,2,1,0:T(1,128)S(1)}, f32[3,2,1,1024]{3,2,1,0:T(1,128)S(1)}, u32[]{:S(2)}, u32[]{:S(2)}) collective-permute-start(f32[3,2,1,1024]{3,2,1,0:T(1,128)S(1)} %get-tuple-element.95), channel_id=1, source_target_pairs={{0,1},{1,2},{2,3},{3,4},{4,5},{5,6},{6,7},{7,8},{8,9},{9,10},{10,1... | collective-permute-start | bytes 73736 | tf_op jit(solution)/shard_map/ppermute | solution.py:18
  107.2 1.0 copy-start.13
  107.3 1.0 copy-start.59
  108.2 19.6 %copy-start.4 = (f32[3,2,8,1024]{3,2,1,0:T(8,128)}, f32[3,2,8,1024]{3,2,1,0:T(8,128)S(1)}, u32[]{:S(2)}) copy-start(f32[3,2,8,1024]{3,2,1,0:T(8,128)S(1)} %slice_add_fusion.3) | copy-start | bytes 589828
  110.5 6.2 %collective-permute-start.22 = (f32[3,2,1,1024]{3,2,1,0:T(1,128)S(1)}, f32[3,2,1,1024]{3,2,1,0:T(1,128)S(1)}, u32[]{:S(2)}, u32[]{:S(2)}) collective-permute-start(f32[3,2,1,1024]{3,2,1,0:T(1,128)S(1)} %get-tuple-element.94), channel_id=1, source_target_pairs={{1,0},{2,1},{3,2},{4,3},{5,4},{6,5},{7,6},{8,7},{9,8},{10,9},{11,1... | collective-permute-start | bytes 73736 | tf_op jit(solution)/shard_map/ppermute | solution.py:21
  112.5 5.1 %collective-permute-start.21 = (f32[3,2,1,1024]{3,2,1,0:T(1,128)S(1)}, f32[3,2,1,1024]{3,2,1,0:T(1,128)S(1)}, u32[]{:S(2)}, u32[]{:S(2)}) collective-permute-start(f32[3,2,1,1024]{3,2,1,0:T(1,128)S(1)} %get-tuple-element.93), channel_id=1, source_target_pairs={{0,1},{1,2},{2,3},{3,4},{4,5},{5,6},{6,7},{7,8},{8,9},{9,10},{10,1... | collective-permute-start | bytes 73736 | tf_op jit(solution)/shard_map/ppermute | solution.py:18
  116.7 1.0 copy-start.11
  116.7 1.0 copy-start.63
  117.7 10.2 %copy-start.5 = (f32[3,2,8,1024]{3,2,1,0:T(8,128)}, f32[3,2,8,1024]{3,2,1,0:T(8,128)S(1)}, u32[]{:S(2)}) copy-start(f32[3,2,8,1024]{3,2,1,0:T(8,128)S(1)} %slice_add_fusion.2) | copy-start | bytes 589828
  120.0 6.2 %collective-permute-start.24 = (f32[3,2,1,1024]{3,2,1,0:T(1,128)S(1)}, f32[3,2,1,1024]{3,2,1,0:T(1,128)S(1)}, u32[]{:S(2)}, u32[]{:S(2)}) collective-permute-start(f32[3,2,1,1024]{3,2,1,0:T(1,128)S(1)} %get-tuple-element.92), channel_id=1, source_target_pairs={{1,0},{2,1},{3,2},{4,3},{5,4},{6,5},{7,6},{8,7},{9,8},{10,9},{11,1... | collective-permute-start | bytes 73736 | tf_op jit(solution)/shard_map/ppermute | solution.py:21
  122.0 5.1 %collective-permute-start.23 = (f32[3,2,1,1024]{3,2,1,0:T(1,128)S(1)}, f32[3,2,1,1024]{3,2,1,0:T(1,128)S(1)}, u32[]{:S(2)}, u32[]{:S(2)}) collective-permute-start(f32[3,2,1,1024]{3,2,1,0:T(1,128)S(1)} %get-tuple-element.91), channel_id=1, source_target_pairs={{0,1},{1,2},{2,3},{3,4},{4,5},{5,6},{6,7},{7,8},{8,9},{9,10},{10,1... | collective-permute-start | bytes 73736 | tf_op jit(solution)/shard_map/ppermute | solution.py:18
  126.2 1.0 copy-start.9
  126.2 1.0 copy-start.62
  127.2 1.1 copy-start.6
  128.0 0.9 copy-start.21
  129.7 7.2 %collective-permute-start.26 = (f32[3,2,1,1024]{3,2,1,0:T(1,128)S(1)}, f32[3,2,1,1024]{3,2,1,0:T(1,128)S(1)}, u32[]{:S(2)}, u32[]{:S(2)}) collective-permute-start(f32[3,2,1,1024]{3,2,1,0:T(1,128)S(1)} %get-tuple-element.90), channel_id=1, source_target_pairs={{1,0},{2,1},{3,2},{4,3},{5,4},{6,5},{7,6},{8,7},{9,8},{10,9},{11,1... | collective-permute-start | bytes 73736 | tf_op jit(solution)/shard_map/ppermute | solution.py:21
  131.6 4.4 %slice-start = ((f32[3,2,8,1024]{3,2,1,0:T(8,128)}), f32[2,2,8,1024]{3,2,1,0:T(8,128)S(1)}, s32[]{:S(2)}) async-start(f32[3,2,8,1024]{3,2,1,0:T(8,128)} %copy-done.2), calls=%async_computation.1 | async-start | bytes 262144 | tf_op jit(solution)/shard_map/slice | solution.py:103
  131.6 4.4 %slice-start.1 = ((f32[3,2,8,1024]{3,2,1,0:T(8,128)}), f32[2,2,8,1024]{3,2,1,0:T(8,128)S(1)}, s32[]{:S(2)}) async-start(f32[3,2,8,1024]{3,2,1,0:T(8,128)} %copy-done.3), calls=%async_computation.2 | async-start | bytes 262144 | tf_op jit(solution)/shard_map/slice | solution.py:103
  131.6 4.4 %slice-start.2 = ((f32[3,2,8,1024]{3,2,1,0:T(8,128)}), f32[2,2,8,1024]{3,2,1,0:T(8,128)S(1)}, s32[]{:S(2)}) async-start(f32[3,2,8,1024]{3,2,1,0:T(8,128)} %copy-done.4), calls=%async_computation.3 | async-start | bytes 262144 | tf_op jit(solution)/shard_map/slice | solution.py:103
  131.6 4.4 %slice-start.3 = ((f32[3,2,8,1024]{3,2,1,0:T(8,128)}), f32[2,2,8,1024]{3,2,1,0:T(8,128)S(1)}, s32[]{:S(2)}) async-start(f32[3,2,8,1024]{3,2,1,0:T(8,128)} %copy-done.5), calls=%async_computation.4 | async-start | bytes 262144 | tf_op jit(solution)/shard_map/slice | solution.py:103
  131.6 4.4 %slice-start.4 = ((f32[3,2,8,1024]{3,2,1,0:T(8,128)}), f32[2,2,8,1024]{3,2,1,0:T(8,128)S(1)}, s32[]{:S(2)}) async-start(f32[3,2,8,1024]{3,2,1,0:T(8,128)} %copy-done.6), calls=%async_computation.5 | async-start | bytes 262144 | tf_op jit(solution)/shard_map/slice | solution.py:103
  131.7 5.3 %collective-permute-start.25 = (f32[3,2,1,1024]{3,2,1,0:T(1,128)S(1)}, f32[3,2,1,1024]{3,2,1,0:T(1,128)S(1)}, u32[]{:S(2)}, u32[]{:S(2)}) collective-permute-start(f32[3,2,1,1024]{3,2,1,0:T(1,128)S(1)} %get-tuple-element.89), channel_id=1, source_target_pairs={{0,1},{1,2},{2,3},{3,4},{4,5},{5,6},{6,7},{7,8},{8,9},{9,10},{10,1... | collective-permute-start | bytes 73736 | tf_op jit(solution)/shard_map/ppermute | solution.py:18
  (81 other events, 58.3 us)
Sparse Core Ops, SparseCore 0:
  137.0 128.1 all-reduce.193
where the time goes:
time: 275 us; the launch traced here: 274 us
  waiting for transfers between devices  132 us (48%)
  starting transfers between devices  87.9 us (32%)
  local copies, waits for them, and re-layouts  21.2 us (8%)
  between operations  16.2 us (6%)
  other arithmetic  16.1 us (6%)
    psum x1, waiting for transfers between devices, local(): grad_forcing = lax.psum(forcing_grad, 'win')  126 us
    ppermute x13, starting transfers between devices, padded_2(): lax.ppermute(lax.slice_in_dim(block, block.shape[dim] - width, None, axis...  49.6 us
    ppermute x13, starting transfers between devices, padded_2(): lax.ppermute(lax.slice_in_dim(block, 0, width, axis=dim), axis, backward)  32.3 us
    unnamed x224, local copies, waits for them, and re-layouts  11.8 us
    ppermute x13, waiting for transfers between devices, padded_2(): lax.ppermute(lax.slice_in_dim(block, block.shape[dim] - width, None, axis...  6.22 us
    ppermute x2, starting transfers between devices, shifted(): return lax.ppermute(array, axis, pairs)  5.93 us
  transfers between devices with their start and end apart: 29, of which 8 were waited for; matrix products, arithmetic and copies ran while one was open for 7% of the time, Pallas kernels for 0%

commit v1 on v0

v1 whole, which is shorter than its diff:
```python
import functools

import jax
import jax.numpy as jnp
from jax import lax
from jax.experimental import pallas as pl
from jax.experimental.pallas import tpu as pltpu
from jax.sharding import PartitionSpec as P

MESH = pl.DeviceIdType.MESH
STEPS = 6
LAT_ROWS = 2048
C_STEP = 0.2
HALF_C = 0.1
OWN = 8
PAD = 7
ROWS = OWN + 2 * PAD
NF = 6
SUB = 8
RW = NF * SUB


def along_x(a):
    ax = a.ndim - 1
    lane = lax.broadcasted_iota(jnp.int32, a.shape, ax)
    up = pltpu.roll(a, 127, ax)
    up = jnp.where(lane == 127, pltpu.roll(up, SUB - 1, ax - 1), up)
    down = pltpu.roll(a, 1, ax)
    down = jnp.where(lane == 0, pltpu.roll(down, 1, ax - 1), down)
    return up - down


def rows_of(ref, first, count, width):
    start = first * (width * SUB)
    if not isinstance(first, int):
        start = pl.multiple_of(start, SUB)
    return ref[pl.ds(start, count * width * SUB), :].reshape(count, width, SUB, 128)


def put_rows(ref, first, width, value):
    start = first * (width * SUB)
    if not isinstance(first, int):
        start = pl.multiple_of(start, SUB)
    count = value.shape[0]
    ref[pl.ds(start, count * width * SUB), :] = value.reshape(count * width * SUB, 128)


def kernel(
    win_n, tile_n, traj, forc, dep, ostep, oval, owt, ew,
    gs_out, gf_out,
    X, F, D, OS, OV, OW, COR, NXT, MU, EARL, LAM, G, GH, LH, RS, RED, AG,
    init_s, init_r, nxt_s, nxt_r, mu_s, mu_r, h_s, h_r, rs_s, rs_r, ag_s, ag_r,
):
    w = lax.axis_index("win")
    t = lax.axis_index("tile")
    y, x = w // 4, lax.rem(w, 4)

    def peer(a, b):
        return lax.rem(y + a, 4) * 4 + lax.rem(x + b, 4)

    peers = [(a, b) for a in range(4) for b in range(4) if a or b]
    peers.sort(key=lambda p: -(min(p[0], 4 - p[0]) + min(p[1], 4 - p[1])))

    barrier = pltpu.get_barrier_semaphore()
    for a, b in peers:
        pl.semaphore_signal(barrier, inc=1, device_id={"win": peer(a, b), "tile": t}, device_id_type=MESH)

    @pl.when(t > 0)
    def _():
        pl.semaphore_signal(barrier, inc=1, device_id={"win": w, "tile": t - 1}, device_id_type=MESH)

    @pl.when(t < tile_n - 1)
    def _():
        pl.semaphore_signal(barrier, inc=1, device_id={"win": w, "tile": t + 1}, device_id_type=MESH)

    for f in range(NF):
        for s in range(SUB):
            cols = pl.ds(128 * s, 128)
            X[0, pl.ds(PAD * RW + f * SUB + s, OWN, stride=RW), :] = traj[0, f // 2, f % 2, :, cols]
            F[pl.ds(PAD * RW + f * SUB + s, OWN, stride=RW), :] = forc[f // 2, f % 2, :, cols]
    for l in range(2):
        for s in range(SUB):
            cols = pl.ds(128 * s, 128)
            D[pl.ds(PAD * 16 + l * SUB + s, OWN, stride=16), :] = dep[l, :, cols]
            OV[pl.ds(PAD * 16 + l * SUB + s, OWN, stride=16), :] = oval[0, l, :, cols]
    for s in range(SUB):
        cols = pl.ds(128 * s, 128)
        OS[pl.ds(PAD * SUB + s, OWN, stride=SUB), :] = ostep[0, :, cols]
        OW[pl.ds(PAD * SUB + s, OWN, stride=SUB), :] = owt[:, cols]

    def clear(ref, first, count, width):
        ref[pl.ds(first * width * SUB, count * width * SUB), :] = jnp.zeros((count * width * SUB, 128), ref.dtype)

    for k in range(STEPS):
        for i in (k, ROWS - 1 - k):
            clear(X.at[k], i, 1, NF)
    clear(D, 0, 1, 2)
    clear(D, ROWS - 1, 1, 2)
    for i in (0, PAD + OWN):
        clear(OS, i, PAD, 1)
        clear(OW, i, PAD, 1)
        clear(OV, i, PAD, 2)
        clear(G, i, PAD, NF)
        clear(LAM.at[0], i, PAD, NF)
        clear(LAM.at[1], i, PAD, NF)

    @pl.when(t == 0)
    def _():
        clear(X.at[0], 1, PAD - 1, NF)
        clear(F, 1, PAD - 1, NF)
        clear(D, 1, PAD - 1, 2)

    @pl.when(t == tile_n - 1)
    def _():
        clear(X.at[0], PAD + OWN, PAD - 1, NF)
        clear(F, PAD + OWN, PAD - 1, NF)
        clear(D, PAD + OWN, PAD - 1, 2)

    band_row = lax.broadcasted_iota(jnp.int32, (24, 128), 0) + (t * OWN - PAD)
    lat = ((LAT_ROWS - tile_n * OWN) // 2 + band_row).astype(jnp.float32)
    COR[...] = (2.0 * C_STEP) * jnp.sin(jnp.pi * ((lat + 0.5) / LAT_ROWS - 0.5))

    def valid(i):
        row = t * OWN - PAD + i
        return jnp.where((row >= 0) & (row < tile_n * OWN), 1.0, 0.0)

    has_low = jnp.where(t > 0, 1, 0)
    has_high = jnp.where(t < tile_n - 1, 1, 0)
    pl.semaphore_wait(barrier, win_n - 1 + has_low + has_high)

    def halo(src, dst, src_row, dst_row, count, width, n, side, sems, tile):
        return pltpu.make_async_remote_copy(
            src_ref=src.at[pl.ds(src_row * width * SUB, count * width * SUB), :],
            dst_ref=dst.at[pl.ds(dst_row * width * SUB, count * width * SUB), :],
            send_sem=sems[0].at[n, side], recv_sem=sems[1].at[n, side],
            device_id={"win": w, "tile": tile}, device_id_type=MESH)

    init = (init_s, init_r)
    ups = [halo(X.at[0], X.at[0], PAD + 2, 1, 6, NF, 0, 0, init, t + 1),
           halo(D, D, PAD + 2, 1, 6, 2, 1, 0, init, t + 1),
           halo(F, F, PAD + 3, 2, 5, NF, 2, 0, init, t + 1)]
    downs = [halo(X.at[0], X.at[0], PAD, PAD + OWN, 6, NF, 0, 1, init, t - 1),
             halo(D, D, PAD, PAD + OWN, 6, 2, 1, 1, init, t - 1),
             halo(F, F, PAD, PAD + OWN, 5, NF, 2, 1, init, t - 1)]

    def to_tiles(ups, downs):
        @pl.when(t < tile_n - 1)
        def _():
            for c in ups:
                c.start()

        @pl.when(t > 0)
        def _():
            for c in downs:
                c.start()

    def from_tiles(ups, downs):
        @pl.when(t > 0)
        def _():
            for c in ups:
                c.wait_recv()

        @pl.when(t < tile_n - 1)
        def _():
            for c in downs:
                c.wait_recv()

    def sent_tiles(ups, downs):
        @pl.when(t < tile_n - 1)
        def _():
            for c in ups:
                c.wait_send()

        @pl.when(t > 0)
        def _():
            for c in downs:
                c.wait_send()

    to_tiles(ups, downs)
    nxt = pltpu.make_async_remote_copy(
        src_ref=X.at[0, pl.ds(PAD * RW, OWN * RW), :], dst_ref=NXT,
        send_sem=nxt_s, recv_sem=nxt_r, device_id={"win": w - 1, "tile": t}, device_id_type=MESH)

    @pl.when(w > 0)
    def _():
        nxt.start()

    from_tiles(ups, downs)

    NB = 2

    def forward(k):
        lo = k + 2

        def block(n, carry):
            i = lo + n * NB
            s = rows_of(X.at[k], i - 1, NB + 2, NF)
            m = rows_of(D, i - 1, NB + 2, 2)
            fo = rows_of(F, i, NB, NF)
            u, v, h = s[:, 0:2], s[:, 2:4], s[:, 4:6]
            p0 = h[:, 0]
            p1 = p0 + h[:, 1]
            mass = m + h
            r = mass * v
            for j in range(NB):
                cor = COR[pl.ds(i + j, 1), :]
                ok = valid(i + j)
                outs = []
                for l in range(2):
                    p = p1 if l else p0
                    uc, vc, hc = u[j + 1, l], v[j + 1, l], h[j + 1, l]
                    nu = uc - HALF_C * (uc * along_x(uc) + vc * (u[j + 2, l] - u[j, l]) + along_x(p[j + 1])) + cor * vc
                    nv = vc - HALF_C * (uc * along_x(vc) + vc * (v[j + 2, l] - v[j, l]) + (p[j + 2] - p[j])) - cor * uc
                    nh = hc - HALF_C * (along_x(mass[j + 1, l] * uc) + (r[j + 2, l] - r[j, l]))
                    outs.append((nu, nv, nh))
                for c in range(3):
                    for l in range(2):
                        f = 2 * c + l
                        put_rows(X.at[k + 1], (i + j) * NF + f, 1, ((outs[l][c] + fo[j, f]) * ok)[None])
            return carry

        lax.fori_loop(0, (ROWS - 2 * lo) // NB, block, 0)

    for k in range(STEPS):
        forward(k)

    not_last = jnp.where(w < win_n - 1, 1.0, 0.0)

    @pl.when(w < win_n - 1)
    def _():
        nxt.wait_recv()

    @pl.when(w == win_n - 1)
    def _():
        NXT[...] = X[STEPS, pl.ds(PAD * RW, OWN * RW), :]

    def end(i, carry):
        nx = rows_of(NXT, i, 1, NF)[0]
        last = rows_of(X.at[STEPS], PAD + i, 1, NF)[0]
        sel = rows_of(OS, PAD + i, 1, 1)[0, 0] == STEPS
        ov = rows_of(OV, PAD + i, 1, 2)[0]
        ow = jnp.where(sel, rows_of(OW, PAD + i, 1, 1)[0, 0], 0.0)
        for f in range(NF):
            mis = (ew[f // 2, f % 2] * not_last) * (nx[f] - last[f])
            put_rows(MU, i * NF + f, 1, mis[None])
            lam = -mis
            if f >= 4:
                lam = lam + ow * (last[f] - ov[f - 4])
            put_rows(LAM.at[0], (PAD + i) * NF + f, 1, lam[None])
            put_rows(G, (PAD + i) * NF + f, 1, lam[None])
        return carry

    lax.fori_loop(0, OWN, end, 0)
    mu = pltpu.make_async_remote_copy(
        src_ref=MU, dst_ref=EARL, send_sem=mu_s, recv_sem=mu_r,
        device_id={"win": w + 1, "tile": t}, device_id_type=MESH)

    @pl.when(w < win_n - 1)
    def _():
        mu.start()

    def backward(k):
        src, dst = (STEPS - k) % 2, (STEPS - k + 1) % 2
        lo = k

        def block(n, carry):
            i = lo + n * NB
            s = rows_of(X.at[k - 1], i - 1, NB + 2, NF)
            lam = rows_of(LAM.at[src], i - 1, NB + 2, NF)
            dp = rows_of(D, i, NB, 2)
            u, v, h = s[:, 0:2], s[:, 2:4], s[:, 4:6]
            a, b, c = lam[:, 0:2], lam[:, 2:4], lam[:, 4:6]
            va, vb = v * a, v * b
            if k > 1:
                os = rows_of(OS, i, NB, 1)
                ov = rows_of(OV, i, NB, 2)
                ow = rows_of(OW, i, NB, 1)
            for j in range(NB):
                cor = COR[pl.ds(i + j, 1), :]
                ok = valid(i + j)
                res = [None] * NF
                grads = []
                for l in range(2):
                    uc, vc, hc = u[j + 1, l], v[j + 1, l], h[j + 1, l]
                    ac, bc, cc = a[j + 1, l], b[j + 1, l], c[j + 1, l]
                    mass = dp[j, l] + hc
                    cx = along_x(cc)
                    cy = c[j + 2, l] - c[j, l]
                    res[l] = ac - cor * bc - HALF_C * (
                        ac * along_x(uc) + bc * along_x(vc) - along_x(uc * ac)
                        - (va[j + 2, l] - va[j, l]) - mass * cx)
                    res[2 + l] = bc + cor * ac - HALF_C * (
                        ac * (u[j + 2, l] - u[j, l]) + bc * (v[j + 2, l] - v[j, l]) - along_x(uc * bc)
                        - (vb[j + 2, l] - vb[j, l]) - mass * cy)
                    grads.append(along_x(ac) + (b[j + 2, l] - b[j, l]))
                    res[4 + l] = cc + HALF_C * (uc * cx + vc * cy)
                res[4] = res[4] + HALF_C * (grads[0] + grads[1])
                res[5] = res[5] + HALF_C * grads[1]
                if k > 1:
                    wt = jnp.where(os[j, 0] == k - 1, ow[j, 0], 0.0)
                    for l in range(2):
                        res[4 + l] = res[4 + l] + wt * (h[j + 1, l] - ov[j, l])
                for f in range(NF):
                    r = (res[f] * ok)[None]
                    put_rows(LAM.at[dst], (i + j) * NF + f, 1, r)
                    if k > 1:
                        old = rows_of(G, (i + j) * NF + f, 1, 1)[0]
                        put_rows(G, (i + j) * NF + f, 1, old + r)
            return carry

        lax.fori_loop(0, (ROWS - 2 * lo) // NB, block, 0)

    for k in range(STEPS, 0, -1):
        backward(k)

    hs = (h_s, h_r)
    gups = [halo(G, GH.at[0], PAD + OWN, 0, 5, NF, 0, 0, hs, t + 1)]
    gdowns = [halo(G, GH.at[1], PAD - 5, 0, 5, NF, 0, 1, hs, t - 1)]
    lups = [halo(LAM.at[0], LH.at[0], PAD + OWN, 0, 6, NF, 1, 0, hs, t + 1)]
    ldowns = [halo(LAM.at[0], LH.at[1], PAD - 6, 0, 6, NF, 1, 1, hs, t - 1)]
    to_tiles(gups + lups, gdowns + ldowns)
    from_tiles(gups, gdowns)

    def add_rows(ref, first, src, count):
        for i in range(count):
            put_rows(ref, first + i, NF, rows_of(ref, first + i, 1, NF) + rows_of(src, i, 1, NF))

    @pl.when(t > 0)
    def _():
        add_rows(G, PAD, GH.at[0], 5)

    @pl.when(t < tile_n - 1)
    def _():
        add_rows(G, PAD + 3, GH.at[1], 5)

    CH = OWN * RW // win_n
    sends = []
    for n, (a, b) in enumerate(peers):
        p = peer(a, b)
        c = pltpu.make_async_remote_copy(
            src_ref=G.at[pl.ds(pl.multiple_of(PAD * RW + p * CH, SUB), CH), :],
            dst_ref=RS.at[pl.ds(n * CH, CH), :],
            send_sem=rs_s.at[n], recv_sem=rs_r.at[n],
            device_id={"win": p, "tile": t}, device_id_type=MESH)
        c.start()
        sends.append(c)
    total = G[pl.ds(pl.multiple_of(PAD * RW + w * CH, SUB), CH), :]
    for c in sends:
        c.wait_recv()
    for n in range(win_n - 1):
        total = total + RS[pl.ds(n * CH, CH), :]
    RED[...] = total
    mine = pl.ds(pl.multiple_of(w * CH, SUB), CH)
    gathers = []
    for n, (a, b) in enumerate(peers):
        c = pltpu.make_async_remote_copy(
            src_ref=RED, dst_ref=AG.at[mine, :],
            send_sem=ag_s.at[n], recv_sem=ag_r.at[n],
            device_id={"win": peer(a, b), "tile": t}, device_id_type=MESH)
        c.start()
        gathers.append(c)
    AG[mine, :] = total

    from_tiles(lups, ldowns)
    first = LAM.at[0]

    @pl.when(t > 0)
    def _():
        add_rows(first, PAD, LH.at[0], 6)

    @pl.when(t < tile_n - 1)
    def _():
        add_rows(first, PAD + 2, LH.at[1], 6)

    @pl.when(w > 0)
    def _():
        mu.wait_recv()

    @pl.when(w == 0)
    def _():
        EARL[...] = jnp.zeros_like(EARL)

    for f in range(NF):
        for s in range(SUB):
            cols = pl.ds(128 * s, 128)
            gs_out[0, f // 2, f % 2, :, cols] = (
                first[pl.ds(PAD * RW + f * SUB + s, OWN, stride=RW), :]
                + EARL[pl.ds(f * SUB + s, OWN, stride=RW), :])

    for c in gathers:
        c.wait_recv()
    for f in range(NF):
        for s in range(SUB):
            gf_out[f // 2, f % 2, :, pl.ds(128 * s, 128)] = AG[pl.ds(f * SUB + s, OWN, stride=RW), :]

    sent_tiles(ups + gups + lups, downs + gdowns + ldowns)

    @pl.when(w > 0)
    def _():
        nxt.wait_send()

    @pl.when(w < win_n - 1)
    def _():
        mu.wait_send()

    for c in sends + gathers:
        c.wait_send()


def solution(mesh):
    win_n, tile_n = mesh.shape["win"], mesh.shape["tile"]

    def local(traj, forc, dep, ostep, oval, owt, ew):
        f32 = jnp.float32

        def flat(rows, width, dtype=f32, lead=()):
            return pltpu.VMEM(lead + (rows * width * SUB, 128), dtype)

        vm = pl.BlockSpec(memory_space=pltpu.VMEM)
        sem = pltpu.SemaphoreType.DMA
        return pl.pallas_call(
            functools.partial(kernel, win_n, tile_n),
            out_shape=(jax.ShapeDtypeStruct(traj.shape, f32), jax.ShapeDtypeStruct(forc.shape, f32)),
            in_specs=[vm] * 6 + [pl.BlockSpec(memory_space=pltpu.SMEM)],
            out_specs=(vm, vm),
            scratch_shapes=[
                flat(ROWS, NF, lead=(STEPS + 1,)),
                flat(ROWS, NF),
                flat(ROWS, 2),
                flat(ROWS, 1, jnp.int32),
                flat(ROWS, 2),
                flat(ROWS, 1),
                pltpu.VMEM((24, 128), f32),
                flat(OWN, NF),
                flat(OWN, NF),
                flat(OWN, NF),
                flat(ROWS, NF, lead=(2,)),
                flat(ROWS, NF),
                flat(5, NF, lead=(2,)),
                flat(6, NF, lead=(2,)),
                flat(OWN, NF),
                pltpu.VMEM((OWN * RW // win_n, 128), f32),
                flat(OWN, NF),
                sem((3, 2)), sem((3, 2)), sem, sem, sem, sem, sem((2, 2)), sem((2, 2)),
                sem((win_n - 1,)), sem((win_n - 1,)), sem((win_n - 1,)), sem((win_n - 1,)),
            ],
            compiler_params=pltpu.CompilerParams(
                collective_id=0, has_side_effects=True, vmem_limit_bytes=40 * 2**20),
        )(traj, forc, dep, ostep, oval, owt, ew)

    return jax.shard_map(
        local,
        mesh=mesh,
        in_specs=(
            P("win", None, None, "tile", None),
            P(None, None, "tile", None),
            P(None, "tile", None),
            P("win", "tile", None),
            P("win", None, "tile", None),
            P("tile", None),
            P(),
        ),
        out_specs=(P("win", None, None, "tile", None), P(None, None, "tile", None)),
        check_vma=False,
    )
```

time: 275 us -> 46.7 us (0.17)
  the two profiles are of different devices: /device:TPU:1 before, /device:TPU:384 now
where the time goes in v1:
time: 46.7 us; the launch traced here: 46.3 us
  Pallas kernels  38.4 us (82%)
  local copies, waits for them, and re-layouts  7.17 us (15%)
  between operations  0.64 us (1%)
    pallas_call x1, Pallas kernels, local(): pl.pallas_call(functools.partial(kernel, win_n, tile_n), out_shape=(jax.S...  38.4 us
    unnamed x15, local copies, waits for them, and re-layouts  7.17 us

profile of v1, /device:TPU:384, one launch (start us, length us, event | category | flops | bytes accessed | tf_op | source)
XLA Modules:
  0.0 46.3 jit_solution(3069037707984007454)
XLA Ops:
  0.6 0.8 %copy.9.ew = f32[3,2]{1,0:T(4,128)S(1)} copy(f32[3,2]{0,1:T(2,128)} %param.13) | data formatting | bytes 48 | tf_op args[6]
  1.4 0.0 copy-start
  1.4 0.9 %copy-done = f32[1,3,2,8,1024]{4,3,2,1,0:T(8,128)S(1)} copy-done((f32[1,3,2,8,1024]{4,3,2,1,0:T(8,128)S(1)}, f32[1,3,2,8,1024]{4,3,2,1,0:T(8,128)}, u32[]{:S(2)}) %copy-start) | copy-done | bytes 196632
  2.3 0.0 copy-start.1
  2.3 0.9 %copy-done.1 = f32[3,2,8,1024]{3,2,1,0:T(8,128)S(1)} copy-done((f32[3,2,8,1024]{3,2,1,0:T(8,128)S(1)}, f32[3,2,8,1024]{3,2,1,0:T(8,128)}, u32[]{:S(2)}) %copy-start.1) | copy-done | bytes 196632
  3.2 0.0 copy-start.2
  3.3 0.8 %copy-done.2 = f32[2,8,1024]{2,1,0:T(8,128)S(1)} copy-done((f32[2,8,1024]{2,1,0:T(8,128)S(1)}, f32[2,8,1024]{2,1,0:T(8,128)}, u32[]{:S(2)}) %copy-start.2) | copy-done | bytes 65560
  4.1 0.0 copy-start.3
  4.1 0.8 %copy-done.3 = f32[1,2,8,1024]{3,2,1,0:T(8,128)S(1)} copy-done((f32[1,2,8,1024]{3,2,1,0:T(8,128)S(1)}, f32[1,2,8,1024]{3,2,1,0:T(8,128)}, u32[]{:S(2)}) %copy-start.3) | copy-done | bytes 65560
  4.9 0.0 copy-start.4
  4.9 0.8 %copy-done.4 = s32[1,8,1024]{2,1,0:T(8,128)S(1)} copy-done((s32[1,8,1024]{2,1,0:T(8,128)S(1)}, s32[1,8,1024]{2,1,0:T(8,128)}, u32[]{:S(2)}) %copy-start.4) | copy-done | bytes 32792
  5.7 0.0 copy-start.5
  5.7 0.8 %copy-done.5 = f32[8,1024]{1,0:T(8,128)S(1)} copy-done((f32[8,1024]{1,0:T(8,128)S(1)}, f32[8,1024]{1,0:T(8,128)}, u32[]{:S(2)}) %copy-start.5) | copy-done | bytes 32792
  6.4 38.4 %shard_map.86 = (f32[1,3,2,8,1024]{4,3,2,1,0:T(8,128)S(1)}, f32[3,2,8,1024]{3,2,1,0:T(8,128)S(1)}) custom-call(f32[1,3,2,8,1024]{4,3,2,1,0:T(8,128)S(1)} %copy-done, f32[3,2,8,1024]{3,2,1,0:T(8,128)S(1)} %copy-done.1, f32[2,8,1024]{2,1,0:T(8,128)S(1)} %copy-done.2, s32[1,8,1024]{2,1,0:T(8,128)S(1)} %copy-done.4, f32[1,2,8,1024]{3,2,1,0:T(8,128)S(1)} %copy-done.3, ...), custom_call_target="tpu_custom_call" | custom-call | tf_op jit(solution)/shard_map/pallas_call | solution.py:421
  44.9 0.7 %copy.12 = f32[1,3,2,8,1024]{4,3,2,1,0:T(8,128)} copy(f32[1,3,2,8,1024]{4,3,2,1,0:T(8,128)S(1)} %get-tuple-element.4) | data formatting | bytes 393216
  45.6 0.7 %copy.13 = f32[3,2,8,1024]{3,2,1,0:T(8,128)} copy(f32[3,2,8,1024]{3,2,1,0:T(8,128)S(1)} %get-tuple-element.5) | data formatting | bytes 393216
Async XLA Ops:
  1.4 0.9 %copy-start = (f32[1,3,2,8,1024]{4,3,2,1,0:T(8,128)S(1)}, f32[1,3,2,8,1024]{4,3,2,1,0:T(8,128)}, u32[]{:S(2)}) copy-start(f32[1,3,2,8,1024]{4,3,2,1,0:T(8,128)} %traj.1) | copy-start | bytes 589828
  2.3 0.9 %copy-start.1 = (f32[3,2,8,1024]{3,2,1,0:T(8,128)S(1)}, f32[3,2,8,1024]{3,2,1,0:T(8,128)}, u32[]{:S(2)}) copy-start(f32[3,2,8,1024]{3,2,1,0:T(8,128)} %forc.1) | copy-start | bytes 589828
  3.2 0.8 %copy-start.2 = (f32[2,8,1024]{2,1,0:T(8,128)S(1)}, f32[2,8,1024]{2,1,0:T(8,128)}, u32[]{:S(2)}) copy-start(f32[2,8,1024]{2,1,0:T(8,128)} %dep.1) | copy-start | bytes 196612
  4.1 0.8 %copy-start.3 = (f32[1,2,8,1024]{3,2,1,0:T(8,128)S(1)}, f32[1,2,8,1024]{3,2,1,0:T(8,128)}, u32[]{:S(2)}) copy-start(f32[1,2,8,1024]{3,2,1,0:T(8,128)} %oval.1) | copy-start | bytes 196612
  4.9 0.8 %copy-start.4 = (s32[1,8,1024]{2,1,0:T(8,128)S(1)}, s32[1,8,1024]{2,1,0:T(8,128)}, u32[]{:S(2)}) copy-start(s32[1,8,1024]{2,1,0:T(8,128)} %ostep.1) | copy-start | bytes 98308
  5.7 0.8 %copy-start.5 = (f32[8,1024]{1,0:T(8,128)S(1)}, f32[8,1024]{1,0:T(8,128)}, u32[]{:S(2)}) copy-start(f32[8,1024]{1,0:T(8,128)} %owt.1) | copy-start | bytes 98308

commit v2 on v0

v2 whole, which is shorter than its diff:
```python
import functools

import jax
import jax.numpy as jnp
from jax import lax
from jax.experimental import pallas as pl
from jax.experimental.pallas import tpu as pltpu
from jax.sharding import PartitionSpec as P

MESH = pl.DeviceIdType.MESH
STEPS = 6
LAT_ROWS = 2048
C_STEP = 0.2
HALF_C = 0.1
OWN = 8
PAD = STEPS
ROWS = OWN + 2 * PAD
NF = 6
SUB = 8
RW = NF * SUB
BW = 14
BR = BW * SUB


def along_x(a):
    lane = lax.broadcasted_iota(jnp.int32, a.shape, 1)
    up = pltpu.roll(a, 127, 1)
    up = jnp.where(lane == 127, pltpu.roll(up, SUB - 1, 0), up)
    down = pltpu.roll(a, 1, 1)
    down = jnp.where(lane == 0, pltpu.roll(down, 1, 0), down)
    return up - down


def get(ref, row, f, width=NF):
    return ref[pl.ds((row * width + f) * SUB, SUB), :]


def put(ref, row, f, value, width=NF):
    ref[pl.ds((row * width + f) * SUB, SUB), :] = value


def less(a, b):
    if a is None:
        return None if b is None else -b
    return a if b is None else a - b


def kernel(
    win_n, tile_n, traj, forc, dep, ostep, oval, owt, ew,
    gs_out, gf_out,
    TT, TF, TD, TS, TV, TW,
    B0, X, DX, OS, OV, OW, COR, NT, NXT, MU, EARL, LAM, G, GH, LH, RS, RED, AG,
    in_s, init_s, init_r, nxt_s, nxt_r, mu_s, mu_r, h_s, h_r, rs_s, rs_r, ag_s, ag_r,
):
    w = lax.axis_index("win")
    t = lax.axis_index("tile")
    y, x = w // 4, lax.rem(w, 4)
    low_tile, high_tile = t > 0, t < tile_n - 1

    def peer(a, b):
        return lax.rem(y + a, 4) * 4 + lax.rem(x + b, 4)

    peers = [(a, b) for a in range(4) for b in range(4) if a or b]
    peers.sort(key=lambda p: -(min(p[0], 4 - p[0]) + min(p[1], 4 - p[1])))

    ins = [pltpu.make_async_copy(src, dst, in_s.at[n]) for n, (src, dst) in enumerate(
        [(traj.at[0], TT), (dep, TD), (forc, TF), (ostep.at[0], TS), (oval.at[0], TV), (owt, TW)])]
    for c in ins:
        c.start()

    barrier = pltpu.get_barrier_semaphore()

    def greet(win, tile):
        pl.semaphore_signal(barrier, inc=1, device_id={"win": win, "tile": tile}, device_id_type=MESH)

    for a, b in peers:
        greet(peer(a, b), t)

    @pl.when(low_tile)
    def _():
        greet(w, t - 1)

    @pl.when(high_tile)
    def _():
        greet(w, t + 1)

    band_row = lax.broadcasted_iota(jnp.int32, (24, 128), 0) + (t * OWN - PAD)
    lat = ((LAT_ROWS - tile_n * OWN) // 2 + band_row).astype(jnp.float32)
    COR[...] = (2.0 * C_STEP) * jnp.sin(jnp.pi * ((lat + 0.5) / LAT_ROWS - 0.5))
    low_ok = jnp.where(low_tile, 1.0, 0.0)
    high_ok = jnp.where(high_tile, 1.0, 0.0)

    @pl.when(t == 0)
    def _():
        B0[pl.ds(0, PAD * BR), :] = jnp.zeros((PAD * BR, 128), jnp.float32)

    @pl.when(t == tile_n - 1)
    def _():
        B0[pl.ds((PAD + OWN) * BR, PAD * BR), :] = jnp.zeros((PAD * BR, 128), jnp.float32)

    def spread(dst, first, width, f, tile):
        for s in range(SUB):
            dst[pl.ds((first * width + f) * SUB + s, OWN, stride=width * SUB), :] = tile(pl.ds(128 * s, 128))

    ins[0].wait()
    for f in range(NF):
        spread(B0, PAD, BW, f, lambda cols: TT[f // 2, f % 2, :, cols])
    ins[1].wait()
    for l in range(2):
        spread(B0, PAD, BW, 6 + l, lambda cols: TD[l, :, cols])
    ins[2].wait()
    for f in range(NF):
        spread(B0, PAD, BW, 8 + f, lambda cols: TF[f // 2, f % 2, :, cols])

    pl.semaphore_wait(barrier, win_n - 1 + jnp.where(low_tile, 1, 0) + jnp.where(high_tile, 1, 0))

    def to_tile(src, src_at, dst, dst_at, size, sems, n, side):
        return pltpu.make_async_remote_copy(
            src_ref=src.at[pl.ds(src_at, size), :], dst_ref=dst.at[pl.ds(dst_at, size), :],
            send_sem=sems[0].at[n, side], recv_sem=sems[1].at[n, side],
            device_id={"win": w, "tile": t + 1 if side == 0 else t - 1}, device_id_type=MESH)

    def init(n, near, count, size):
        up = (PAD + OWN - near - count + 1) * BR, (PAD - near - count + 1) * BR
        down = (PAD + near - 1) * BR, (PAD + OWN + near - 1) * BR
        return [to_tile(B0, a, B0, b, size, (init_s, init_r), n, side) for side, (a, b) in enumerate((up, down))]

    first = [init(0, 1, 2, 2 * BR), init(1, 3, 2, 2 * BR), init(2, 5, 1, BR), init(3, 6, 1, SUB * SUB)]

    def start(pairs):
        @pl.when(high_tile)
        def _():
            for c in pairs:
                c[0].start()

        @pl.when(low_tile)
        def _():
            for c in pairs:
                c[1].start()

    def arrive(pairs):
        @pl.when(low_tile)
        def _():
            for c in pairs:
                c[0].wait_recv()

        @pl.when(high_tile)
        def _():
            for c in pairs:
                c[1].wait_recv()

    def left(pairs):
        @pl.when(high_tile)
        def _():
            for c in pairs:
                c[0].wait_send()

        @pl.when(low_tile)
        def _():
            for c in pairs:
                c[1].wait_send()

    start(first)
    nxt = pltpu.make_async_remote_copy(
        src_ref=TT, dst_ref=NT, send_sem=nxt_s, recv_sem=nxt_r,
        device_id={"win": w - 1, "tile": t}, device_id_type=MESH)

    @pl.when(w > 0)
    def _():
        nxt.start()

    def state(k, r, f):
        return get(B0, PAD + r, f, BW) if k == 0 else get(X.at[k - 1], PAD + r, f)

    def side_ok(r):
        return low_ok if r < 0 else high_ok if r >= OWN else None

    def forward(k, blocks):
        outs = []
        for block in blocks:
            near = range(block[0] - 1, block[-1] + 2)
            s = {r: [state(k, r, f) for f in range(NF)] for r in near}
            p = {r: (s[r][4], s[r][4] + s[r][5]) for r in near}
            mass = {r: [get(B0, PAD + r, 6 + l, BW) + s[r][4 + l] for l in range(2)] for r in near}
            q = {r: [mass[r][l] * s[r][2 + l] for l in range(2)] for r in near}
            for r in block:
                cor = COR[pl.ds(PAD + r, 1), :]
                new, dx = [None] * NF, [None] * 4
                lo, hi = r - 1, r + 1
                for l in range(2):
                    u, v, h = s[r][l], s[r][2 + l], s[r][4 + l]
                    dx[l], dx[2 + l] = along_x(u), along_x(v)
                    new[l] = u - HALF_C * (u * dx[l] + v * (s[hi][l] - s[lo][l]) + along_x(p[r][l])) + cor * v
                    new[2 + l] = v - HALF_C * (
                        u * dx[2 + l] + v * (s[hi][2 + l] - s[lo][2 + l]) + (p[hi][l] - p[lo][l])) - cor * u
                    new[4 + l] = h - HALF_C * (along_x(mass[r][l] * u) + (q[hi][l] - q[lo][l]))
                ok = side_ok(r)
                for f in range(NF):
                    new[f] = new[f] + get(B0, PAD + r, 8 + f, BW)
                    if ok is not None:
                        new[f] = new[f] * ok
                outs.append((r, new, dx))
        for r, new, dx in outs:
            for f in range(NF):
                put(X.at[k], PAD + r, f, new[f])
            for f in range(4):
                put(DX.at[k], PAD + r, f, dx[f], 4)

    for k in range(3):
        forward(k, [range(1 + k, OWN - 1 - k)])
    for n, near in enumerate((1, 3, 5)):
        arrive([first[n]] if n < 2 else first[2:])
        if n == 0:
            for c in ins[3:]:
                c.wait()
            spread(OS, 0, 1, 0, lambda cols: TS[:, cols])
            spread(OW, 0, 1, 0, lambda cols: TW[:, cols])
            for l in range(2):
                spread(OV, 0, 2, l, lambda cols: TV[l, :, cols])
        for k in range(STEPS):
            low = [r for r in (k - near, k - near + 1) if r < OWN // 2]
            high = [OWN - 1 - r for r in reversed(low)]
            if low:
                forward(k, [low, high])

    not_last = jnp.where(w < win_n - 1, 1.0, 0.0)

    @pl.when(w < win_n - 1)
    def _():
        nxt.wait_recv()

    @pl.when(w == win_n - 1)
    def _():
        NT[...] = jnp.zeros_like(NT)

    for f in range(NF):
        spread(NXT, 0, NF, f, lambda cols: NT[f // 2, f % 2, :, cols])

    def pull(k, r, l):
        ow = jnp.where(get(OS, r, 0, 1) == k, get(OW, r, 0, 1), 0.0)
        return ow * (state(k, r, 4 + l) - get(OV, r, l, 2))

    for r in range(OWN):
        for f in range(NF):
            mis = (ew[f % 2, f // 2] * not_last) * (get(NXT, r, f) - state(STEPS, r, f))
            put(MU, r, f, mis)
            lam = -mis
            if f >= 4:
                lam = lam + pull(STEPS, r, f - 4)
            put(LAM.at[0], PAD + r, f, lam)
            put(G, PAD + r, f, lam)
    mu = pltpu.make_async_remote_copy(
        src_ref=MU, dst_ref=EARL, send_sem=mu_s, recv_sem=mu_r,
        device_id={"win": w + 1, "tile": t}, device_id_type=MESH)

    @pl.when(w < win_n - 1)
    def _():
        mu.start()

    def backward(k, rows):
        src, dst = LAM.at[(STEPS - k) % 2], LAM.at[(STEPS - k + 1) % 2]
        reach = STEPS - k
        none = [None] * NF
        near = range(rows[0] - 1, rows[-1] + 2)
        lam = {r: [get(src, PAD + r, f) for f in range(NF)] if -reach <= r < OWN + reach else none for r in near}
        s = {r: [state(k - 1, r, f) for f in range(NF)] for r in near if -reach - 1 <= r < OWN + reach + 1}

        def times(r, l, c):
            return None if lam[r][c] is None else s[r][2 + l] * lam[r][c]

        va = {r: [times(r, l, l) for l in range(2)] for r in near}
        vb = {r: [times(r, l, 2 + l) for l in range(2)] for r in near}
        outs = []
        for r in rows:
            lo, hi = r - 1, r + 1
            new, grads = [None] * NF, [None] * 2
            cor = COR[pl.ds(PAD + r, 1), :]
            for l in range(2):
                u, v, h = s[r][l], s[r][2 + l], s[r][4 + l]
                a, b, c = lam[r][l], lam[r][2 + l], lam[r][4 + l]
                mass = get(B0, PAD + r, 6 + l, BW) + h
                cy = less(lam[hi][4 + l], lam[lo][4 + l])
                ya, yb = less(va[hi][l], va[lo][l]), less(vb[hi][l], vb[lo][l])
                by = less(lam[hi][2 + l], lam[lo][2 + l])
                if a is None:
                    new[l] = HALF_C * ya
                    new[2 + l] = HALF_C * (yb + mass * cy)
                    new[4 + l] = HALF_C * (v * cy)
                    grads[l] = by
                    continue
                cx = along_x(c)
                dxu, dxv = get(DX.at[k - 1], PAD + r, l, 4), get(DX.at[k - 1], PAD + r, 2 + l, 4)
                new[l] = a - cor * b - HALF_C * (a * dxu + b * dxv - along_x(u * a) - ya - mass * cx)
                new[2 + l] = b + cor * a - HALF_C * (
                    a * (s[hi][l] - s[lo][l]) + b * (s[hi][2 + l] - s[lo][2 + l]) - along_x(u * b) - yb - mass * cy)
                new[4 + l] = c + HALF_C * (u * cx + v * cy)
                grads[l] = along_x(a) + by
            new[4] = new[4] + HALF_C * (grads[0] + grads[1])
            new[5] = new[5] + HALF_C * grads[1]
            ok = side_ok(r)
            if k > 1 and ok is None:
                for l in range(2):
                    new[4 + l] = new[4 + l] + pull(k - 1, r, l)
            if ok is not None:
                new = [value * ok for value in new]
            outs.append((r, new))
        for r, new in outs:
            fresh = r == -reach - 1 or r == OWN + reach
            for f in range(NF):
                put(dst, PAD + r, f, new[f])
                if k > 1:
                    put(G, PAD + r, f, new[f] if fresh else get(G, PAD + r, f) + new[f])

    for k in range(STEPS, 0, -1):
        reach = STEPS - k + 1
        half = OWN // 2 + reach
        backward(k, range(-reach, half - reach))
        backward(k, range(half - reach, OWN + reach))

    CH = OWN * RW // win_n

    def chunk(p):
        return pl.ds(pl.multiple_of(PAD * RW + p * CH, SUB), CH)

    g_halo = [
        to_tile(G, (PAD + OWN) * RW, GH.at[0], 0, (PAD - 1) * RW, (h_s, h_r), 1, 0),
        to_tile(G, RW, GH.at[1], 0, (PAD - 1) * RW, (h_s, h_r), 1, 1)]
    start([g_halo])
    arrive([g_halo])

    def add_halo(at, src):
        span = pl.ds(at * RW, (PAD - 1) * RW)
        G[span, :] = G[span, :] + src[...]

    @pl.when(low_tile)
    def _():
        add_halo(PAD, GH.at[0])

    @pl.when(high_tile)
    def _():
        add_halo(PAD + OWN - PAD + 1, GH.at[1])

    for n, (a, b) in enumerate(peers):
        p = peer(a, b)
        pltpu.make_async_remote_copy(
            src_ref=G.at[chunk(p), :], dst_ref=RS.at[pl.ds(n * CH, CH), :], send_sem=rs_s, recv_sem=rs_r,
            device_id={"win": p, "tile": t}, device_id_type=MESH).start()

    lam_halo = [
        to_tile(LAM.at[0], (PAD + OWN) * RW, LH.at[0], 0, PAD * RW, (h_s, h_r), 0, 0),
        to_tile(LAM.at[0], 0, LH.at[1], 0, PAD * RW, (h_s, h_r), 0, 1)]
    start([lam_halo])

    def all_of(ref, count, sem):
        part = ref.at[pl.ds(0, count * CH), :]
        pltpu.make_async_copy(part, part, sem).wait()

    all_of(RS, win_n - 1, rs_r)
    total = G[chunk(w), :]
    for n in range(win_n - 1):
        total = total + RS[pl.ds(n * CH, CH), :]
    RED[...] = total

    mine = pl.ds(pl.multiple_of(w * CH, SUB), CH)
    for a, b in peers:
        pltpu.make_async_remote_copy(
            src_ref=RED, dst_ref=AG.at[mine, :], send_sem=ag_s, recv_sem=ag_r,
            device_id={"win": peer(a, b), "tile": t}, device_id_type=MESH).start()
    AG[mine, :] = RED[...]

    arrive([lam_halo])

    def add_rows(at, src):
        span = pl.ds(at * RW, PAD * RW)
        LAM[0, span, :] = LAM[0, span, :] + src[...]

    @pl.when(low_tile)
    def _():
        add_rows(PAD, LH.at[0])

    @pl.when(high_tile)
    def _():
        add_rows(PAD + OWN - PAD, LH.at[1])

    @pl.when(w > 0)
    def _():
        mu.wait_recv()

    @pl.when(w == 0)
    def _():
        EARL[...] = jnp.zeros_like(EARL)

    def gather(src, first, f, s):
        return src[pl.ds((first * NF + f) * SUB + s, OWN, stride=RW), :]

    for f in range(NF):
        for s in range(SUB):
            gs_out[0, f // 2, f % 2, :, pl.ds(128 * s, 128)] = (
                gather(LAM.at[0], PAD, f, s) + gather(EARL, 0, f, s))

    all_of(AG, win_n - 1, ag_r)
    for f in range(NF):
        for s in range(SUB):
            gf_out[f // 2, f % 2, :, pl.ds(128 * s, 128)] = gather(AG, 0, f, s)

    left(first + [lam_halo, g_halo])

    @pl.when(w > 0)
    def _():
        nxt.wait_send()

    @pl.when(w < win_n - 1)
    def _():
        mu.wait_send()

    all_of(RS, win_n - 1, rs_s)
    all_of(RS, win_n - 1, ag_s)


def solution(mesh):
    win_n, tile_n = mesh.shape["win"], mesh.shape["tile"]

    def local(traj, forc, dep, ostep, oval, owt, ew):
        f32 = jnp.float32

        def flat(rows, width, dtype=f32, lead=()):
            return pltpu.VMEM(lead + (rows * width * SUB, 128), dtype)

        vm = pl.BlockSpec(memory_space=pltpu.VMEM)
        hbm = pl.BlockSpec(memory_space=pl.ANY)
        sem = pltpu.SemaphoreType.DMA
        return pl.pallas_call(
            functools.partial(kernel, win_n, tile_n),
            out_shape=(jax.ShapeDtypeStruct(traj.shape, f32), jax.ShapeDtypeStruct(forc.shape, f32)),
            in_specs=[hbm] * 6 + [pl.BlockSpec(memory_space=pltpu.SMEM)],
            out_specs=(vm, vm),
            scratch_shapes=[
                pltpu.VMEM(traj.shape[1:], f32), pltpu.VMEM(forc.shape, f32), pltpu.VMEM(dep.shape, f32),
                pltpu.VMEM(ostep.shape[1:], jnp.int32), pltpu.VMEM(oval.shape[1:], f32),
                pltpu.VMEM(owt.shape, f32),
                flat(ROWS, BW),
                flat(ROWS, NF, lead=(STEPS,)),
                flat(ROWS, 4, lead=(STEPS,)),
                flat(OWN + 1, 1, jnp.int32),
                flat(OWN + 1, 2),
                flat(OWN + 1, 1),
                pltpu.VMEM((24, 128), f32),
                pltpu.VMEM(traj.shape[1:], f32),
                flat(OWN + 1, NF),
                flat(OWN, NF),
                flat(OWN, NF),
                flat(ROWS, NF, lead=(2,)),
                flat(ROWS, NF),
                flat(PAD - 1, NF, lead=(2,)),
                flat(PAD, NF, lead=(2,)),
                flat(OWN, NF),
                pltpu.VMEM((OWN * RW // win_n, 128), f32),
                flat(OWN, NF),
                sem((6,)), sem((4, 2)), sem((4, 2)), sem, sem, sem, sem, sem((2, 2)), sem((2, 2)),
                sem, sem, sem, sem,
            ],
            compiler_params=pltpu.CompilerParams(
                collective_id=0, has_side_effects=True, vmem_limit_bytes=60 * 2**20),
        )(traj, forc, dep, ostep, oval, owt, ew.T)

    return jax.shard_map(
        local,
        mesh=mesh,
        in_specs=(
            P("win", None, None, "tile", None),
            P(None, None, "tile", None),
            P(None, "tile", None),
            P("win", "tile", None),
            P("win", None, "tile", None),
            P("tile", None),
            P(),
        ),
        out_specs=(P("win", None, None, "tile", None), P(None, None, "tile", None)),
        check_vma=False,
    )
```

time: 275 us -> 34 us (0.12)
  waiting for transfers between devices: 132 us -> 0 us
  starting transfers between devices: 87.9 us -> 0 us
  Pallas kernels: 0 us -> 30.7 us
  local copies, waits for them, and re-layouts: 21.2 us -> 2.34 us
  other arithmetic: 16.1 us -> 0 us
  between operations: 16.2 us -> 0.65 us
    psum x1 -> x0, waiting for transfers between devices: 126 us -> none  [local(): grad_forcing = lax.psum(forcing_grad, 'win')]
    ppermute x28 -> x0, starting transfers between devices: 87.9 us -> none  [the longest x13 49.6 us: padded_2(): lax.ppermute(lax.slice_in_dim(block, block.shape[dim] - width, None, axis...]
    pallas_call x0 -> x1, Pallas kernels: none -> 30.7 us  [local(): pl.pallas_call(functools.partial(kernel, win_n, tile_n), out_shape=(jax.S...]
    unnamed x224 -> x4, local copies, waits for them, and re-layouts: 11.8 us -> 2.34 us
    ppermute x28 -> x0, waiting for transfers between devices: 6.26 us -> none  [the longest x13 6.22 us: padded_2(): lax.ppermute(lax.slice_in_dim(block, block.shape[dim] - width, None, axis...]
    slice x64 -> x0, local copies, waits for them, and re-layouts: 5.5 us -> none  [the longest x46 3.61 us: along_x(): return 0.5 * (jnp.roll(field, -1, axis=-1) - jnp.roll(field, 1, axis=-1))]
    another operation x29 -> x0, other arithmetic: 3.97 us -> none  [the longest x12 2.13 us: advance(): pressure = jnp.cumsum(height, axis=0)]
    split x72 -> x0, local copies, waits for them, and re-layouts: 3.66 us -> none  [along_x(): return 0.5 * (jnp.roll(field, -1, axis=-1) - jnp.roll(field, 1, axis=-1))]
  transfers between devices with their start and end apart: 29 -> 0, of which waited for: 8 -> 0; matrix products, arithmetic and copies ran while one was open for 7% -> 0% of each run, Pallas kernels for 0% -> 0%
where the time goes in v2:
time: 34 us; the launch traced here: 33.7 us
  Pallas kernels  30.7 us (90%)
  local copies, waits for them, and re-layouts  2.34 us (7%)
  between operations  0.65 us (2%)
    pallas_call x1, Pallas kernels, local(): pl.pallas_call(functools.partial(kernel, win_n, tile_n), out_shape=(jax.S...  30.7 us
    unnamed x4, local copies, waits for them, and re-layouts  2.34 us

profile of v2, /device:TPU:1, one launch (start us, length us, event | category | flops | bytes accessed | tf_op | source)
XLA Modules:
  0.0 33.7 jit_solution(2600625642041497859)
XLA Ops:
  0.6 30.7 %shard_map.86 = (f32[1,3,2,8,1024]{4,3,2,1,0:T(8,128)}, f32[3,2,8,1024]{3,2,1,0:T(8,128)}) custom-call(f32[1,3,2,8,1024]{4,3,2,1,0:T(8,128)} %traj.1, f32[3,2,8,1024]{3,2,1,0:T(8,128)} %forc.1, f32[2,8,1024]{2,1,0:T(8,128)} %dep.1, s32[1,8,1024]{2,1,0:T(8,128)} %ostep.1, f32[1,2,8,1024]{3,2,1,0:T(8,128)} %oval.1, f32[8,1024]{1,0:T(8,128)} %owt.1, f32[2,3]{1,0:T(2,128)} %bitcast.1), custom_call_target="tpu_custom_call" | custom-call | tf_op jit(solution)/shard_map/pallas_call | solution.py:432
  31.3 0.0 copy-start
  31.3 1.7 %copy.11 = f32[1,3,2,8,1024]{4,3,2,1,0:T(8,128)} copy(f32[1,3,2,8,1024]{4,3,2,1,0:T(8,128)} %get-tuple-element.4) | data formatting | bytes 393216
  33.0 0.0 copy-done
  33.0 0.7 %copy.12 = f32[3,2,8,1024]{3,2,1,0:T(8,128)} copy(f32[3,2,8,1024]{3,2,1,0:T(8,128)S(1)} %copy-done) | data formatting | bytes 393216
Async XLA Ops:
  31.3 1.7 %copy-start = (f32[3,2,8,1024]{3,2,1,0:T(8,128)S(1)}, f32[3,2,8,1024]{3,2,1,0:T(8,128)}, u32[]{:S(2)}) copy-start(f32[3,2,8,1024]{3,2,1,0:T(8,128)} %get-tuple-element.5) | copy-start | bytes 589828

commit v3 on v2

--- a/solution.py
+++ b/solution.py
@@ -46,9 +46,9 @@
 
 
 def kernel(
-    win_n, tile_n, traj, forc, dep, ostep, oval, owt, ew,
+    win_n, tile_n, traj, forc, dep, ostep, oval, owt, ew_in,
     gs_out, gf_out,
-    TT, TF, TD, TS, TV, TW,
+    TT, TF, TD, TS, TV, TW, ew,
     B0, X, DX, OS, OV, OW, COR, NT, NXT, MU, EARL, LAM, G, GH, LH, RS, RED, AG,
     in_s, init_s, init_r, nxt_s, nxt_r, mu_s, mu_r, h_s, h_r, rs_s, rs_r, ag_s, ag_r,
 ):
@@ -64,7 +64,7 @@
     peers.sort(key=lambda p: -(min(p[0], 4 - p[0]) + min(p[1], 4 - p[1])))
 
     ins = [pltpu.make_async_copy(src, dst, in_s.at[n]) for n, (src, dst) in enumerate(
-        [(traj.at[0], TT), (dep, TD), (forc, TF), (ostep.at[0], TS), (oval.at[0], TV), (owt, TW)])]
+        [(traj.at[0], TT), (dep, TD), (forc, TF), (ostep.at[0], TS), (oval.at[0], TV), (owt, TW), (ew_in, ew)])]
     for c in ins:
         c.start()
 
@@ -258,7 +258,7 @@
         mu.start()
 
     def backward(k, rows):
-        src, dst = LAM.at[(STEPS - k) % 2], LAM.at[(STEPS - k + 1) % 2]
+        src, dst = LAM.at[STEPS - k], LAM.at[STEPS - k + 1]
         reach = STEPS - k
         none = [None] * NF
         near = range(rows[0] - 1, rows[-1] + 2)
@@ -311,21 +311,30 @@
                 if k > 1:
                     put(G, PAD + r, f, new[f] if fresh else get(G, PAD + r, f) + new[f])
 
-    for k in range(STEPS, 0, -1):
+    backward(STEPS, range(-1, OWN + 1))
+    for k in range(STEPS - 1, 1, -1):
         reach = STEPS - k + 1
-        half = OWN // 2 + reach
-        backward(k, range(-reach, half - reach))
-        backward(k, range(half - reach, OWN + reach))
-
-    CH = OWN * RW // win_n
-
-    def chunk(p):
-        return pl.ds(pl.multiple_of(PAD * RW + p * CH, SUB), CH)
-
+        backward(k, range(-reach, k - 2))
+        backward(k, range(OWN + 2 - k, OWN + reach))
     g_halo = [
         to_tile(G, (PAD + OWN) * RW, GH.at[0], 0, (PAD - 1) * RW, (h_s, h_r), 1, 0),
         to_tile(G, RW, GH.at[1], 0, (PAD - 1) * RW, (h_s, h_r), 1, 1)]
     start([g_halo])
+    for k in range(STEPS - 1, 1, -1):
+        backward(k, range(k - 2, OWN + 2 - k))
+    backward(1, range(-STEPS, OWN // 2))
+    backward(1, range(OWN // 2, OWN + STEPS))
+    last = LAM.at[STEPS]
+    lam_halo = [
+        to_tile(last, (PAD + OWN) * RW, LH.at[0], 0, PAD * RW, (h_s, h_r), 0, 0),
+        to_tile(last, 0, LH.at[1], 0, PAD * RW, (h_s, h_r), 0, 1)]
+    start([lam_halo])
+
+    CH = OWN * RW // win_n
+
+    def chunk(p):
+        return pl.ds(pl.multiple_of(PAD * RW + p * CH, SUB), CH)
+
     arrive([g_halo])
 
     def add_halo(at, src):
@@ -345,11 +354,6 @@
         pltpu.make_async_remote_copy(
             src_ref=G.at[chunk(p), :], dst_ref=RS.at[pl.ds(n * CH, CH), :], send_sem=rs_s, recv_sem=rs_r,
             device_id={"win": p, "tile": t}, device_id_type=MESH).start()
-
-    lam_halo = [
-        to_tile(LAM.at[0], (PAD + OWN) * RW, LH.at[0], 0, PAD * RW, (h_s, h_r), 0, 0),
-        to_tile(LAM.at[0], 0, LH.at[1], 0, PAD * RW, (h_s, h_r), 0, 1)]
-    start([lam_halo])
 
     def all_of(ref, count, sem):
         part = ref.at[pl.ds(0, count * CH), :]
@@ -372,7 +376,7 @@
 
     def add_rows(at, src):
         span = pl.ds(at * RW, PAD * RW)
-        LAM[0, span, :] = LAM[0, span, :] + src[...]
+        last[span, :] = last[span, :] + src[...]
 
     @pl.when(low_tile)
     def _():
@@ -396,7 +400,7 @@
     for f in range(NF):
         for s in range(SUB):
             gs_out[0, f // 2, f % 2, :, pl.ds(128 * s, 128)] = (
-                gather(LAM.at[0], PAD, f, s) + gather(EARL, 0, f, s))
+                gather(last, PAD, f, s) + gather(EARL, 0, f, s))
 
     all_of(AG, win_n - 1, ag_r)
     for f in range(NF):
@@ -417,6 +421,14 @@
     all_of(RS, win_n - 1, ag_s)
 
 
+def hand_over(a, b, a_out, b_out, sems):
+    copies = [pltpu.make_async_copy(src, dst, sems.at[n]) for n, (src, dst) in enumerate([(a, a_out), (b, b_out)])]
+    for c in copies:
+        c.start()
+    for c in copies:
+        c.wait()
+
+
 def solution(mesh):
     win_n, tile_n = mesh.shape["win"], mesh.shape["tile"]
 
@@ -427,17 +439,17 @@
             return pltpu.VMEM(lead + (rows * width * SUB, 128), dtype)
 
         vm = pl.BlockSpec(memory_space=pltpu.VMEM)
-        hbm = pl.BlockSpec(memory_space=pl.ANY)
+        hbm = pl.BlockSpec(memory_space=pltpu.HBM)
         sem = pltpu.SemaphoreType.DMA
-        return pl.pallas_call(
+        results = pl.pallas_call(
             functools.partial(kernel, win_n, tile_n),
             out_shape=(jax.ShapeDtypeStruct(traj.shape, f32), jax.ShapeDtypeStruct(forc.shape, f32)),
-            in_specs=[hbm] * 6 + [pl.BlockSpec(memory_space=pltpu.SMEM)],
+            in_specs=[hbm] * 7,
             out_specs=(vm, vm),
             scratch_shapes=[
                 pltpu.VMEM(traj.shape[1:], f32), pltpu.VMEM(forc.shape, f32), pltpu.VMEM(dep.shape, f32),
                 pltpu.VMEM(ostep.shape[1:], jnp.int32), pltpu.VMEM(oval.shape[1:], f32),
-                pltpu.VMEM(owt.shape, f32),
+                pltpu.VMEM(owt.shape, f32), pltpu.SMEM((2, 3), f32),
                 flat(ROWS, BW),
                 flat(ROWS, NF, lead=(STEPS,)),
                 flat(ROWS, 4, lead=(STEPS,)),
@@ -449,19 +461,27 @@
                 flat(OWN + 1, NF),
                 flat(OWN, NF),
                 flat(OWN, NF),
-                flat(ROWS, NF, lead=(2,)),
+                flat(ROWS, NF, lead=(STEPS + 1,)),
                 flat(ROWS, NF),
                 flat(PAD - 1, NF, lead=(2,)),
                 flat(PAD, NF, lead=(2,)),
                 flat(OWN, NF),
                 pltpu.VMEM((OWN * RW // win_n, 128), f32),
                 flat(OWN, NF),
-                sem((6,)), sem((4, 2)), sem((4, 2)), sem, sem, sem, sem, sem((2, 2)), sem((2, 2)),
+                sem((7,)), sem((4, 2)), sem((4, 2)), sem, sem, sem, sem, sem((2, 2)), sem((2, 2)),
                 sem, sem, sem, sem,
             ],
             compiler_params=pltpu.CompilerParams(
-                collective_id=0, has_side_effects=True, vmem_limit_bytes=60 * 2**20),
-        )(traj, forc, dep, ostep, oval, owt, ew.T)
+                collective_id=0, has_side_effects=True, vmem_limit_bytes=16 * 2**20),
+        )(*[pltpu.with_memory_space_constraint(z, pltpu.HBM) for z in (traj, forc, dep, ostep, oval, owt, ew.T)])
+        out = pl.BlockSpec(memory_space=pl.ANY)
+        return pl.pallas_call(
+            hand_over,
+            out_shape=[jax.ShapeDtypeStruct(r.shape, f32) for r in results],
+            in_specs=[out] * 2,
+            out_specs=[out] * 2,
+            scratch_shapes=[sem((2,))],
+        )(*results)
 
     return jax.shard_map(
         local,

time: 34 us -> 44.5 us (1.31)
  Pallas kernels: 30.7 us -> 42.4 us
  local copies, waits for them, and re-layouts: 2.34 us -> 1.34 us
    pallas_call x0 -> x1, Pallas kernels: none -> 13 us  [local(): pl.pallas_call(hand_over, out_shape=[jax.ShapeDtypeStruct(r.shape, f32) f...]
    pallas_call x1, Pallas kernels: 30.7 us -> 29.4 us  [local(): pl.pallas_call(functools.partial(kernel, win_n, tile_n), out_shape=(jax.S...]
    unnamed x4, local copies, waits for them, and re-layouts: 2.34 us -> 1.34 us
where the time goes in v3:
time: 44.5 us; the launch traced here: 44.4 us
  Pallas kernels  42.4 us (95%)
  local copies, waits for them, and re-layouts  1.34 us (3%)
  between operations  0.65 us (1%)
    pallas_call x1, Pallas kernels, local(): pl.pallas_call(functools.partial(kernel, win_n, tile_n), out_shape=(jax.S...  29.4 us
    pallas_call x1, Pallas kernels, local(): pl.pallas_call(hand_over, out_shape=[jax.ShapeDtypeStruct(r.shape, f32) f...  13 us
    unnamed x4, local copies, waits for them, and re-layouts  1.34 us

profile of v3, /device:TPU:1, one launch (start us, length us, event | category | flops | bytes accessed | tf_op | source)
XLA Modules:
  0.0 44.4 jit_solution(6654624343996148595)
XLA Ops:
  0.6 29.4 %shard_map.86 = (f32[1,3,2,8,1024]{4,3,2,1,0:T(8,128)S(1)}, f32[3,2,8,1024]{3,2,1,0:T(8,128)S(1)}) custom-call(f32[1,3,2,8,1024]{4,3,2,1,0:T(8,128)} %traj.1, f32[3,2,8,1024]{3,2,1,0:T(8,128)} %forc.1, f32[2,8,1024]{2,1,0:T(8,128)} %dep.1, s32[1,8,1024]{2,1,0:T(8,128)} %ostep.1, f32[1,2,8,1024]{3,2,1,0:T(8,128)} %oval.1, f32[8,1024]{1,0:T(8,128)} %owt.1, ...), custom_call_target="tpu_custom_call" | custom-call | tf_op jit(solution)/shard_map/pallas_call | solution.py:444
  30.0 0.0 copy-start
  30.0 0.7 %copy-done = f32[1,3,2,8,1024]{4,3,2,1,0:T(8,128)} copy-done((f32[1,3,2,8,1024]{4,3,2,1,0:T(8,128)}, f32[1,3,2,8,1024]{4,3,2,1,0:T(8,128)S(1)}, u32[]{:S(2)}) %copy-start) | copy-done | bytes 196632
  30.7 0.0 copy-start.1
  30.7 0.7 %copy-done.1 = f32[3,2,8,1024]{3,2,1,0:T(8,128)} copy-done((f32[3,2,8,1024]{3,2,1,0:T(8,128)}, f32[3,2,8,1024]{3,2,1,0:T(8,128)S(1)}, u32[]{:S(2)}) %copy-start.1) | copy-done | bytes 196632
  31.4 13.0 %shard_map.87 = (f32[1,3,2,8,1024]{4,3,2,1,0:T(8,128)}, f32[3,2,8,1024]{3,2,1,0:T(8,128)}) custom-call(f32[1,3,2,8,1024]{4,3,2,1,0:T(8,128)} %copy-done, f32[3,2,8,1024]{3,2,1,0:T(8,128)} %copy-done.1), custom_call_target="tpu_custom_call" | custom-call | tf_op jit(solution)/shard_map/pallas_call | solution.py:478
Async XLA Ops:
  30.0 0.7 %copy-start = (f32[1,3,2,8,1024]{4,3,2,1,0:T(8,128)}, f32[1,3,2,8,1024]{4,3,2,1,0:T(8,128)S(1)}, u32[]{:S(2)}) copy-start(f32[1,3,2,8,1024]{4,3,2,1,0:T(8,128)S(1)} %get-tuple-element.4.a) | copy-start | bytes 589828
  30.7 0.7 %copy-start.1 = (f32[3,2,8,1024]{3,2,1,0:T(8,128)}, f32[3,2,8,1024]{3,2,1,0:T(8,128)S(1)}, u32[]{:S(2)}) copy-start(f32[3,2,8,1024]{3,2,1,0:T(8,128)S(1)} %get-tuple-element.5.b) | copy-start | bytes 589828

commit v4 on v3

--- a/solution.py
+++ b/solution.py
@@ -421,14 +421,6 @@
     all_of(RS, win_n - 1, ag_s)
 
 
-def hand_over(a, b, a_out, b_out, sems):
-    copies = [pltpu.make_async_copy(src, dst, sems.at[n]) for n, (src, dst) in enumerate([(a, a_out), (b, b_out)])]
-    for c in copies:
-        c.start()
-    for c in copies:
-        c.wait()
-
-
 def solution(mesh):
     win_n, tile_n = mesh.shape["win"], mesh.shape["tile"]
 
@@ -441,7 +433,7 @@
         vm = pl.BlockSpec(memory_space=pltpu.VMEM)
         hbm = pl.BlockSpec(memory_space=pltpu.HBM)
         sem = pltpu.SemaphoreType.DMA
-        results = pl.pallas_call(
+        return pl.pallas_call(
             functools.partial(kernel, win_n, tile_n),
             out_shape=(jax.ShapeDtypeStruct(traj.shape, f32), jax.ShapeDtypeStruct(forc.shape, f32)),
             in_specs=[hbm] * 7,
@@ -474,14 +466,6 @@
             compiler_params=pltpu.CompilerParams(
                 collective_id=0, has_side_effects=True, vmem_limit_bytes=16 * 2**20),
         )(*[pltpu.with_memory_space_constraint(z, pltpu.HBM) for z in (traj, forc, dep, ostep, oval, owt, ew.T)])
-        out = pl.BlockSpec(memory_space=pl.ANY)
-        return pl.pallas_call(
-            hand_over,
-            out_shape=[jax.ShapeDtypeStruct(r.shape, f32) for r in results],
-            in_specs=[out] * 2,
-            out_specs=[out] * 2,
-            scratch_shapes=[sem((2,))],
-        )(*results)
 
     return jax.shard_map(
         local,

time: 44.5 us -> 31.5 us (0.71)
  Pallas kernels: 42.4 us -> 29.4 us
    pallas_call x1 -> x0, Pallas kernels: 13 us -> none  [local(): pl.pallas_call(hand_over, out_shape=[jax.ShapeDtypeStruct(r.shape, f32) f...]
    unnamed x4 -> x2, local copies, waits for them, and re-layouts: 1.34 us -> 1.36 us
where the time goes in v4:
time: 31.5 us; the launch traced here: 31.4 us
  Pallas kernels  29.4 us (93%)
  local copies, waits for them, and re-layouts  1.36 us (4%)
  between operations  0.64 us (2%)
    pallas_call x1, Pallas kernels, local(): pl.pallas_call(functools.partial(kernel, win_n, tile_n), out_shape=(jax.S...  29.4 us
    unnamed x2, local copies, waits for them, and re-layouts  1.36 us

profile of v4, /device:TPU:1, one launch (start us, length us, event | category | flops | bytes accessed | tf_op | source)
XLA Modules:
  0.0 31.4 jit_solution(12953861432447307274)
XLA Ops:
  0.6 29.4 %shard_map.86 = (f32[1,3,2,8,1024]{4,3,2,1,0:T(8,128)S(1)}, f32[3,2,8,1024]{3,2,1,0:T(8,128)S(1)}) custom-call(f32[1,3,2,8,1024]{4,3,2,1,0:T(8,128)} %traj.1, f32[3,2,8,1024]{3,2,1,0:T(8,128)} %forc.1, f32[2,8,1024]{2,1,0:T(8,128)} %dep.1, s32[1,8,1024]{2,1,0:T(8,128)} %ostep.1, f32[1,2,8,1024]{3,2,1,0:T(8,128)} %oval.1, f32[8,1024]{1,0:T(8,128)} %owt.1, ...), custom_call_target="tpu_custom_call" | custom-call | tf_op jit(solution)/shard_map/pallas_call | solution.py:436
  30.0 0.7 %copy.11 = f32[1,3,2,8,1024]{4,3,2,1,0:T(8,128)} copy(f32[1,3,2,8,1024]{4,3,2,1,0:T(8,128)S(1)} %get-tuple-element.4) | data formatting | bytes 393216
  30.7 0.7 %copy.12 = f32[3,2,8,1024]{3,2,1,0:T(8,128)} copy(f32[3,2,8,1024]{3,2,1,0:T(8,128)S(1)} %get-tuple-element.5) | data formatting | bytes 393216

commit v5 on v3

--- a/solution.py
+++ b/solution.py
@@ -15,6 +15,7 @@
 OWN = 8
 PAD = STEPS
 ROWS = OWN + 2 * PAD
+GP = OWN
 NF = 6
 SUB = 8
 RW = NF * SUB
@@ -49,9 +50,10 @@
     win_n, tile_n, traj, forc, dep, ostep, oval, owt, ew_in,
     gs_out, gf_out,
     TT, TF, TD, TS, TV, TW, ew,
-    B0, X, DX, OS, OV, OW, COR, NT, NXT, MU, EARL, LAM, G, GH, LH, RS, RED, AG,
-    in_s, init_s, init_r, nxt_s, nxt_r, mu_s, mu_r, h_s, h_r, rs_s, rs_r, ag_s, ag_r,
+    B0, X, DX, OS, OV, OW, COR, NT, NXT, MU, EARL, LAM, G, LH, RS, RED, AG,
+    in_s, init_s, init_r, nxt_s, nxt_r, mu_s, mu_r, h_s, h_r, rs_s0, rs_s1, rs_s2, rs_r0, rs_r1, rs_r2, ag_s, ag_r,
 ):
+    rs_s, rs_r = (rs_s0, rs_s1, rs_s2), (rs_r0, rs_r1, rs_r2)
     w = lax.axis_index("win")
     t = lax.axis_index("tile")
     y, x = w // 4, lax.rem(w, 4)
@@ -63,26 +65,36 @@
     peers = [(a, b) for a in range(4) for b in range(4) if a or b]
     peers.sort(key=lambda p: -(min(p[0], 4 - p[0]) + min(p[1], 4 - p[1])))
 
+    barrier = pltpu.get_barrier_semaphore()
+
+    def greet(win, tile):
+        pl.semaphore_signal(barrier, inc=1, device_id={"win": win, "tile": tile}, device_id_type=MESH)
+
+    @pl.when(low_tile)
+    def _():
+        greet(w, t - 1)
+
+    @pl.when(high_tile)
+    def _():
+        greet(w, t + 1)
+
     ins = [pltpu.make_async_copy(src, dst, in_s.at[n]) for n, (src, dst) in enumerate(
         [(traj.at[0], TT), (dep, TD), (forc, TF), (ostep.at[0], TS), (oval.at[0], TV), (owt, TW), (ew_in, ew)])]
     for c in ins:
         c.start()
 
-    barrier = pltpu.get_barrier_semaphore()
-
-    def greet(win, tile):
-        pl.semaphore_signal(barrier, inc=1, device_id={"win": win, "tile": tile}, device_id_type=MESH)
-
     for a, b in peers:
         greet(peer(a, b), t)
 
     @pl.when(low_tile)
     def _():
-        greet(w, t - 1)
+        for a, b in peers:
+            greet(peer(a, b), t - 1)
 
     @pl.when(high_tile)
     def _():
-        greet(w, t + 1)
+        for a, b in peers:
+            greet(peer(a, b), t + 1)
 
     band_row = lax.broadcasted_iota(jnp.int32, (24, 128), 0) + (t * OWN - PAD)
     lat = ((LAT_ROWS - tile_n * OWN) // 2 + band_row).astype(jnp.float32)
@@ -112,7 +124,7 @@
     for f in range(NF):
         spread(B0, PAD, BW, 8 + f, lambda cols: TF[f // 2, f % 2, :, cols])
 
-    pl.semaphore_wait(barrier, win_n - 1 + jnp.where(low_tile, 1, 0) + jnp.where(high_tile, 1, 0))
+    pl.semaphore_wait(barrier, win_n - 1 + jnp.where(low_tile, win_n, 0) + jnp.where(high_tile, win_n, 0))
 
     def to_tile(src, src_at, dst, dst_at, size, sems, n, side):
         return pltpu.make_async_remote_copy(
@@ -248,7 +260,7 @@
             if f >= 4:
                 lam = lam + pull(STEPS, r, f - 4)
             put(LAM.at[0], PAD + r, f, lam)
-            put(G, PAD + r, f, lam)
+            put(G, GP + r, f, lam)
     mu = pltpu.make_async_remote_copy(
         src_ref=MU, dst_ref=EARL, send_sem=mu_s, recv_sem=mu_r,
         device_id={"win": w + 1, "tile": t}, device_id_type=MESH)
@@ -309,19 +321,54 @@
             for f in range(NF):
                 put(dst, PAD + r, f, new[f])
                 if k > 1:
-                    put(G, PAD + r, f, new[f] if fresh else get(G, PAD + r, f) + new[f])
+                    put(G, GP + r, f, new[f] if fresh else get(G, GP + r, f) + new[f])
 
     backward(STEPS, range(-1, OWN + 1))
     for k in range(STEPS - 1, 1, -1):
         reach = STEPS - k + 1
         backward(k, range(-reach, k - 2))
         backward(k, range(OWN + 2 - k, OWN + reach))
-    g_halo = [
-        to_tile(G, (PAD + OWN) * RW, GH.at[0], 0, (PAD - 1) * RW, (h_s, h_r), 1, 0),
-        to_tile(G, RW, GH.at[1], 0, (PAD - 1) * RW, (h_s, h_r), 1, 1)]
-    start([g_halo])
+    CH = OWN * RW // win_n
+    HALO = 2 * (STEPS - 1)
+    mine = pl.ds(pl.multiple_of(w * CH, SUB), CH)
+
+    SIZE = OWN * RW
+
+    def add_up(at, p, tile, group, n):
+        pltpu.make_async_remote_copy(
+            src_ref=G.at[pl.ds(pl.multiple_of(GP * RW + at, SUB), CH), :],
+            dst_ref=RS.at[pl.ds(group * SIZE + n * CH, CH), :],
+            send_sem=rs_s[group], recv_sem=rs_r[group],
+            device_id={"win": p, "tile": tile}, device_id_type=MESH).start()
+
+    every = peers + [(0, 0)]
+
+    def up_to(n, p):
+        @pl.when(p < HALO)
+        def _():
+            add_up(SIZE + p * CH, p, t + 1, 1, n)
+
+    def down_to(n, p):
+        @pl.when(p >= win_n - HALO)
+        def _():
+            add_up(p * CH - SIZE, p, t - 1, 2, n)
+
+    @pl.when(high_tile)
+    def _():
+        for n, (a, b) in enumerate(every):
+            up_to(n, peer(a, b))
+
+    @pl.when(low_tile)
+    def _():
+        for n, (a, b) in enumerate(every):
+            down_to(n, peer(a, b))
+
     for k in range(STEPS - 1, 1, -1):
         backward(k, range(k - 2, OWN + 2 - k))
+
+    for n, (a, b) in enumerate(peers):
+        p = peer(a, b)
+        add_up(p * CH, p, t, 0, n)
     backward(1, range(-STEPS, OWN // 2))
     backward(1, range(OWN // 2, OWN + STEPS))
     last = LAM.at[STEPS]
@@ -330,42 +377,32 @@
         to_tile(last, 0, LH.at[1], 0, PAD * RW, (h_s, h_r), 0, 1)]
     start([lam_halo])
 
-    CH = OWN * RW // win_n
-
-    def chunk(p):
-        return pl.ds(pl.multiple_of(PAD * RW + p * CH, SUB), CH)
-
-    arrive([g_halo])
-
-    def add_halo(at, src):
-        span = pl.ds(at * RW, (PAD - 1) * RW)
-        G[span, :] = G[span, :] + src[...]
-
-    @pl.when(low_tile)
-    def _():
-        add_halo(PAD, GH.at[0])
-
-    @pl.when(high_tile)
-    def _():
-        add_halo(PAD + OWN - PAD + 1, GH.at[1])
-
-    for n, (a, b) in enumerate(peers):
-        p = peer(a, b)
-        pltpu.make_async_remote_copy(
-            src_ref=G.at[chunk(p), :], dst_ref=RS.at[pl.ds(n * CH, CH), :], send_sem=rs_s, recv_sem=rs_r,
-            device_id={"win": p, "tile": t}, device_id_type=MESH).start()
-
     def all_of(ref, count, sem):
         part = ref.at[pl.ds(0, count * CH), :]
         pltpu.make_async_copy(part, part, sem).wait()
 
-    all_of(RS, win_n - 1, rs_r)
-    total = G[chunk(w), :]
-    for n in range(win_n - 1):
-        total = total + RS[pl.ds(n * CH, CH), :]
-    RED[...] = total
-
-    mine = pl.ds(pl.multiple_of(w * CH, SUB), CH)
+    def take(group, count):
+        all_of(RS, count, rs_r[group])
+        total = RED[...]
+        for n in range(count):
+            total = total + RS[pl.ds(group * SIZE + n * CH, CH), :]
+        RED[...] = total
+
+    RED[...] = G[pl.ds(pl.multiple_of(GP * RW + w * CH, SUB), CH), :]
+    take(0, win_n - 1)
+
+    @pl.when(low_tile)
+    def _():
+        @pl.when(w < HALO)
+        def _():
+            take(1, win_n)
+
+    @pl.when(high_tile)
+    def _():
+        @pl.when(w >= win_n - HALO)
+        def _():
+            take(2, win_n)
+
     for a, b in peers:
         pltpu.make_async_remote_copy(
             src_ref=RED, dst_ref=AG.at[mine, :], send_sem=ag_s, recv_sem=ag_r,
@@ -407,7 +444,7 @@
         for s in range(SUB):
             gf_out[f // 2, f % 2, :, pl.ds(128 * s, 128)] = gather(AG, 0, f, s)
 
-    left(first + [lam_halo, g_halo])
+    left(first + [lam_halo])
 
     @pl.when(w > 0)
     def _():
@@ -417,7 +454,16 @@
     def _():
         mu.wait_send()
 
-    all_of(RS, win_n - 1, rs_s)
+    all_of(RS, win_n - 1, rs_s[0])
+
+    @pl.when(high_tile)
+    def _():
+        all_of(RS, HALO, rs_s[1])
+
+    @pl.when(low_tile)
+    def _():
+        all_of(RS, HALO, rs_s[2])
+
     all_of(RS, win_n - 1, ag_s)
 
 
@@ -462,24 +508,22 @@
                 flat(OWN, NF),
                 flat(OWN, NF),
                 flat(ROWS, NF, lead=(STEPS + 1,)),
-                flat(ROWS, NF),
-                flat(PAD - 1, NF, lead=(2,)),
+                flat(OWN + 2 * GP, NF),
                 flat(PAD, NF, lead=(2,)),
-                flat(OWN, NF),
+                flat(3 * OWN, NF),
                 pltpu.VMEM((OWN * RW // win_n, 128), f32),
                 flat(OWN, NF),
-                sem((7,)), sem((4, 2)), sem((4, 2)), sem, sem, sem, sem, sem((2, 2)), sem((2, 2)),
-                sem, sem, sem, sem,
+                sem((7,)), sem((4, 2)), sem((4, 2)), sem, sem, sem, sem, sem((1, 2)), sem((1, 2)),
+                sem, sem, sem, sem, sem, sem, sem, sem,
             ],
             compiler_params=pltpu.CompilerParams(
                 collective_id=0, has_side_effects=True, vmem_limit_bytes=16 * 2**20),
         )(*[pltpu.with_memory_space_constraint(z, pltpu.HBM) for z in (traj, forc, dep, ostep, oval, owt, ew.T)])
-        out = pl.BlockSpec(memory_space=pl.ANY)
         return pl.pallas_call(
             hand_over,
             out_shape=[jax.ShapeDtypeStruct(r.shape, f32) for r in results],
-            in_specs=[out] * 2,
-            out_specs=[out] * 2,
+            in_specs=[vm] * 2,
+            out_specs=[hbm] * 2,
             scratch_shapes=[sem((2,))],
         )(*results)
 

time: 44.5 us -> 36.2 us (0.81)
  the two profiles are of different devices: /device:TPU:1 before, /device:TPU:258 now
where the time goes in v5:
time: 36.2 us; the launch traced here: 36.1 us
  Pallas kernels  34.1 us (94%)
  local copies, waits for them, and re-layouts  1.34 us (4%)
  between operations  0.65 us (2%)
    pallas_call x1, Pallas kernels, local(): pl.pallas_call(functools.partial(kernel, win_n, tile_n), out_shape=(jax.S...  32.3 us
    pallas_call x1, Pallas kernels, local(): pl.pallas_call(hand_over, out_shape=[jax.ShapeDtypeStruct(r.shape, f32) f...  1.78 us
    unnamed x4, local copies, waits for them, and re-layouts  1.34 us

profile of v5, /device:TPU:258, one launch (start us, length us, event | category | flops | bytes accessed | tf_op | source)
XLA Modules:
  0.0 36.1 jit_solution(3103610797720859483)
XLA Ops:
  0.6 32.3 %shard_map.86 = (f32[1,3,2,8,1024]{4,3,2,1,0:T(8,128)S(1)}, f32[3,2,8,1024]{3,2,1,0:T(8,128)S(1)}) custom-call(f32[1,3,2,8,1024]{4,3,2,1,0:T(8,128)} %traj.1, f32[3,2,8,1024]{3,2,1,0:T(8,128)} %forc.1, f32[2,8,1024]{2,1,0:T(8,128)} %dep.1, s32[1,8,1024]{2,1,0:T(8,128)} %ostep.1, f32[1,2,8,1024]{3,2,1,0:T(8,128)} %oval.1, f32[8,1024]{1,0:T(8,128)} %owt.1, ...), custom_call_target="tpu_custom_call" | custom-call | tf_op jit(solution)/shard_map/pallas_call | solution.py:490
  32.9 0.0 copy-start
  33.0 0.7 %copy-done = f32[1,3,2,8,1024]{4,3,2,1,0:T(8,128)} copy-done((f32[1,3,2,8,1024]{4,3,2,1,0:T(8,128)}, f32[1,3,2,8,1024]{4,3,2,1,0:T(8,128)S(1)}, u32[]{:S(2)}) %copy-start) | copy-done | bytes 196632
  33.6 0.0 copy-start.1
  33.6 0.7 %copy-done.1 = f32[3,2,8,1024]{3,2,1,0:T(8,128)} copy-done((f32[3,2,8,1024]{3,2,1,0:T(8,128)}, f32[3,2,8,1024]{3,2,1,0:T(8,128)S(1)}, u32[]{:S(2)}) %copy-start.1) | copy-done | bytes 196632
  34.3 1.8 %shard_map.87 = (f32[1,3,2,8,1024]{4,3,2,1,0:T(8,128)}, f32[3,2,8,1024]{3,2,1,0:T(8,128)}) custom-call(f32[1,3,2,8,1024]{4,3,2,1,0:T(8,128)} %copy-done, f32[3,2,8,1024]{3,2,1,0:T(8,128)} %copy-done.1), custom_call_target="tpu_custom_call" | custom-call | tf_op jit(solution)/shard_map/pallas_call | solution.py:522
Async XLA Ops:
  32.9 0.7 %copy-start = (f32[1,3,2,8,1024]{4,3,2,1,0:T(8,128)}, f32[1,3,2,8,1024]{4,3,2,1,0:T(8,128)S(1)}, u32[]{:S(2)}) copy-start(f32[1,3,2,8,1024]{4,3,2,1,0:T(8,128)S(1)} %get-tuple-element.4.a) | copy-start | bytes 589828
  33.6 0.7 %copy-start.1 = (f32[3,2,8,1024]{3,2,1,0:T(8,128)}, f32[3,2,8,1024]{3,2,1,0:T(8,128)S(1)}, u32[]{:S(2)}) copy-start(f32[3,2,8,1024]{3,2,1,0:T(8,128)S(1)} %get-tuple-element.5.b) | copy-start | bytes 589828

commit v6 on v4

--- a/solution.py
+++ b/solution.py
@@ -63,26 +63,26 @@
     peers = [(a, b) for a in range(4) for b in range(4) if a or b]
     peers.sort(key=lambda p: -(min(p[0], 4 - p[0]) + min(p[1], 4 - p[1])))
 
+    barrier = pltpu.get_barrier_semaphore()
+
+    def greet(win, tile):
+        pl.semaphore_signal(barrier, inc=1, device_id={"win": win, "tile": tile}, device_id_type=MESH)
+
+    @pl.when(low_tile)
+    def _():
+        greet(w, t - 1)
+
+    @pl.when(high_tile)
+    def _():
+        greet(w, t + 1)
+
     ins = [pltpu.make_async_copy(src, dst, in_s.at[n]) for n, (src, dst) in enumerate(
         [(traj.at[0], TT), (dep, TD), (forc, TF), (ostep.at[0], TS), (oval.at[0], TV), (owt, TW), (ew_in, ew)])]
     for c in ins:
         c.start()
 
-    barrier = pltpu.get_barrier_semaphore()
-
-    def greet(win, tile):
-        pl.semaphore_signal(barrier, inc=1, device_id={"win": win, "tile": tile}, device_id_type=MESH)
-
     for a, b in peers:
         greet(peer(a, b), t)
-
-    @pl.when(low_tile)
-    def _():
-        greet(w, t - 1)
-
-    @pl.when(high_tile)
-    def _():
-        greet(w, t + 1)
 
     band_row = lax.broadcasted_iota(jnp.int32, (24, 128), 0) + (t * OWN - PAD)
     lat = ((LAT_ROWS - tile_n * OWN) // 2 + band_row).astype(jnp.float32)
@@ -335,25 +335,44 @@
     def chunk(p):
         return pl.ds(pl.multiple_of(PAD * RW + p * CH, SUB), CH)
 
-    arrive([g_halo])
-
     def add_halo(at, src):
         span = pl.ds(at * RW, (PAD - 1) * RW)
         G[span, :] = G[span, :] + src[...]
 
-    @pl.when(low_tile)
-    def _():
+    def from_low():
+        g_halo[0].wait_recv()
         add_halo(PAD, GH.at[0])
 
-    @pl.when(high_tile)
-    def _():
+    def from_high():
+        g_halo[1].wait_recv()
         add_halo(PAD + OWN - PAD + 1, GH.at[1])
 
-    for n, (a, b) in enumerate(peers):
-        p = peer(a, b)
+    def to_sum(p, n):
         pltpu.make_async_remote_copy(
             src_ref=G.at[chunk(p), :], dst_ref=RS.at[pl.ds(n * CH, CH), :], send_sem=rs_s, recv_sem=rs_r,
             device_id={"win": p, "tile": t}, device_id_type=MESH).start()
+
+    def to_sums(wanted):
+        for n, (a, b) in enumerate(peers):
+            p = peer(a, b)
+            pl.when(wanted(p))(functools.partial(to_sum, p, n))
+
+    alone = 2 * (OWN - (PAD - 1))
+    core = lax.rem(t, 2)
+
+    @pl.when(core == 0)
+    def _():
+        from_high()
+        to_sums(lambda p: p >= win_n - alone)
+        pl.when(low_tile)(from_low)
+        to_sums(lambda p: p < win_n - alone)
+
+    @pl.when(core == 1)
+    def _():
+        from_low()
+        to_sums(lambda p: p < alone)
+        pl.when(high_tile)(from_high)
+        to_sums(lambda p: p >= alone)
 
     def all_of(ref, count, sem):
         part = ref.at[pl.ds(0, count * CH), :]

time: 31.5 us -> 31.1 us (0.987)
  Pallas kernels: 29.4 us -> 29 us
    pallas_call x1, Pallas kernels: 29.4 us -> 29 us  [local(): pl.pallas_call(functools.partial(kernel, win_n, tile_n), out_shape=(jax.S...]
where the time goes in v6:
time: 31.1 us; the launch traced here: 31 us
  Pallas kernels  29 us (93%)
  local copies, waits for them, and re-layouts  1.36 us (4%)
  between operations  0.64 us (2%)
    pallas_call x1, Pallas kernels, local(): pl.pallas_call(functools.partial(kernel, win_n, tile_n), out_shape=(jax.S...  29 us
    unnamed x2, local copies, waits for them, and re-layouts  1.36 us

profile of v6, /device:TPU:1, one launch (start us, length us, event | category | flops | bytes accessed | tf_op | source)
XLA Modules:
  0.0 31.0 jit_solution(15760771823984449347)
XLA Ops:
  0.6 29.0 %shard_map.86 = (f32[1,3,2,8,1024]{4,3,2,1,0:T(8,128)S(1)}, f32[3,2,8,1024]{3,2,1,0:T(8,128)S(1)}) custom-call(f32[1,3,2,8,1024]{4,3,2,1,0:T(8,128)} %traj.1, f32[3,2,8,1024]{3,2,1,0:T(8,128)} %forc.1, f32[2,8,1024]{2,1,0:T(8,128)} %dep.1, s32[1,8,1024]{2,1,0:T(8,128)} %ostep.1, f32[1,2,8,1024]{3,2,1,0:T(8,128)} %oval.1, f32[8,1024]{1,0:T(8,128)} %owt.1, ...), custom_call_target="tpu_custom_call" | custom-call | tf_op jit(solution)/shard_map/pallas_call | solution.py:455
  29.6 0.7 %copy.11 = f32[1,3,2,8,1024]{4,3,2,1,0:T(8,128)} copy(f32[1,3,2,8,1024]{4,3,2,1,0:T(8,128)S(1)} %get-tuple-element.4) | data formatting | bytes 393216
  30.3 0.7 %copy.12 = f32[3,2,8,1024]{3,2,1,0:T(8,128)} copy(f32[3,2,8,1024]{3,2,1,0:T(8,128)S(1)} %get-tuple-element.5) | data formatting | bytes 393216
